TPU v7x, 512 devices: a whole 4x8x8 slice. The times are simulated.
512 devices in a mesh: dir: 16 (over y, x_lo), space: 32 (over z, x_hi, core).
Axes of the slice: x: 4 (x_hi: 2, x_lo: 2; x = x_hi * 2 + x_lo), y: 8, z: 8, core: 2. Of those that a mesh axis runs over, the one named last changes fastest.
Arguments:
- velocity: float32 [16, 3, 256, 16, 512], P('dir', None, 'space'), may hold values from -6 to 6
- precursor: float32 [16, 3, 256, 512], P('dir', None, 'space'), may hold values from -6 to 6
- rot_map: int32 [16, 256, 512], P('dir', 'space'), may hold values from 0 to 131071, as said below
- facade_cell: int32 [16, 8192], P('dir', 'space'), may hold values from 0 to 65535
- facade_owner: int32 [16, 8192, 1], P('dir', 'space'), may hold values from 0 to 31; in each aligned block of 256 rows (0 to 255, 256 to 511, ..., all dimensions but the last counted through in order) at most 24 rows name the same one
- facade_panel: int32 [16, 8192], P('dir', 'space'), may hold values from 0 to 127
- facade_area: float32 [16, 8192], P('dir', 'space'), may hold values from 0.2 to 2
Outputs:
- velocity_new: float32 [16, 3, 256, 16, 512], P('dir', None, 'space')
- potential: float32 [16, 256, 16, 512], P('dir', 'space')
- panel_force: float32 [16, 4096], P('dir', 'space')
Inputs may be any that keep to these rules, and one draw needn't show every extreme that they name: rot_map[d, y, z] = q_d(y) * 512 + z, where q_d is a permutation of the 256 spanwise rows, drawn for each direction. `facade_owner`: among the 256 facade cells of one device at most 24 have the same owner.
All inputs are finite; a program needn't handle non-finite values.
Results may differ from a plain program's by a relative error of at most 0.00002.
Values sent between devices are 32-bit elements; how exact they have to be, the bound alone decides.
A program may use at most 192 MiB of HBM per device.

v0:
```python
import jax
import jax.numpy as jnp
from jax import lax
from jax.sharding import PartitionSpec as P

ITERS = 20
PAN_DEV = 128
time_step = 0.12
viscosity = 0.2


def extended_2(cells, sides, width):
    for axis, dim in sides:
        count = lax.axis_size(axis)
        ends = count - 1
        head = lax.slice_in_dim(cells, 0, width, axis=dim)
        tail = lax.slice_in_dim(cells, cells.shape[dim] - width, cells.shape[dim], axis=dim)
        cells = jnp.concatenate(
            [
                lax.ppermute(tail, axis, [(i, (i + 1) % count) for i in range(ends)]),
                cells,
                lax.ppermute(head, axis, [((i + 1) % count, i) for i in range(ends)]),
            ],
            axis=dim,
        )
    return cells


def spread(block, axis, holder):
    block = jnp.where(lax.axis_index(axis) == holder, block, jnp.zeros_like(block))
    return lax.psum(block, axis)


def pad_edges(field):
    lead = field.ndim - 3
    widths = [(0, 0)] * lead
    padded = jnp.pad(field, widths + [(0, 0), (0, 0), (1, 1)])
    return jnp.pad(padded, widths + [(0, 0), (1, 1), (0, 0)], mode="edge")


def tentative(extended):
    q = pad_edges(extended)
    centre = q[:, 1:-1, 1:-1, 1:-1]
    xplus = q[:, 1:-1, 2:, 1:-1]
    xminus = q[:, 1:-1, :-2, 1:-1]
    zplus = q[:, 1:-1, 1:-1, 2:]
    zminus = q[:, 1:-1, 1:-1, :-2]
    yplus = q[:, 2:, 1:-1, 1:-1]
    yminus = q[:, :-2, 1:-1, 1:-1]
    lap = xplus + xminus + zplus + zminus + 16.0 * (yplus + yminus) - 36.0 * centre
    advect = (
        centre[0] * (xplus - xminus) * 0.5
        + centre[1] * (yplus - yminus) * 2.0
        + centre[2] * (zplus - zminus) * 0.5
    )
    return centre + time_step * (viscosity * lap - advect)


def divergence(extended):
    q = pad_edges(extended)
    along_x = (q[0, 1:-1, 2:, 1:-1] - q[0, 1:-1, :-2, 1:-1]) * 0.5
    along_y = (q[1, 2:, 1:-1, 1:-1] - q[1, :-2, 1:-1, 1:-1]) * 2.0
    along_z = (q[2, 1:-1, 1:-1, 2:] - q[2, 1:-1, 1:-1, :-2]) * 0.5
    return along_x + along_y + along_z


def relax_sweep(extended, source):
    q = jnp.pad(extended, ((0, 0), (1, 1), (1, 1)))
    total = q[1:-1, 2:, 1:-1] + q[1:-1, :-2, 1:-1] + q[1:-1, 1:-1, 2:] + q[1:-1, 1:-1, :-2]
    total = total + 16.0 * (q[2:, 1:-1, 1:-1] + q[:-2, 1:-1, 1:-1])
    return (total - source) / 36.0


def gradient(extended):
    q = jnp.pad(extended, ((0, 0), (1, 1), (1, 1)))
    grad_x = (q[1:-1, 2:, 1:-1] - q[1:-1, :-2, 1:-1]) * 0.5
    grad_y = (q[2:, 1:-1, 1:-1] - q[:-2, 1:-1, 1:-1]) * 2.0
    grad_z = (q[1:-1, 1:-1, 2:] - q[1:-1, 1:-1, :-2]) * 0.5
    return jnp.stack([grad_x, grad_y, grad_z])


def extend(field, width):
    return extended_2(field, (("space", 0),), width)


def inside_rows(first, count, span):
    global_rows = first + jnp.arange(count, dtype=jnp.int32)
    return (global_rows >= 0) & (global_rows < span)


def body(velocity, precursor, rot_map, facade_cell, facade_owner, facade_panel, facade_area):
    groups = lax.axis_size("space")
    rows = velocity.shape[2]
    stream = velocity.shape[3]
    height = velocity.shape[4]
    span = rows * groups
    start = lax.axis_index("space") * rows
    plane_piece = spread(precursor, "dir", 0)
    plane = lax.all_gather(plane_piece[0], "space", axis=1, tiled=True)
    flat_plane = plane.reshape(3, span * height)
    inflow = jnp.take(flat_plane, rot_map[0].reshape(-1), axis=1).reshape(3, rows, height)
    field = velocity[0].at[:, :, 0, :].set(inflow)
    sweeps_each = 1
    widened = extended_2(field, (("space", 1),), sweeps_each + 1)
    ustar_wide = tentative(widened)
    keep = inside_rows(start - sweeps_each, rows + 2 * sweeps_each, span)
    ustar_wide = jnp.where(keep[None, :, None, None], ustar_wide, 0.0)
    ustar = ustar_wide[:, sweeps_each : sweeps_each + rows]
    source_wide = divergence(ustar_wide)
    empty = jnp.zeros((rows, stream, height), jnp.float32)

    def one_round(step, phi):
        current = extend(phi, sweeps_each)
        current = relax_sweep(current, source_wide)
        return current

    phi = lax.fori_loop(0, ITERS // sweeps_each, one_round, empty)
    moved = ustar - gradient(extend(phi, 1))
    values = facade_area[0] * phi.reshape(-1)[facade_cell[0]]
    owners = facade_owner[0, :, 0]
    panels = facade_panel[0]
    panel_count = PAN_DEV
    terms = (
        jnp.zeros((groups * panel_count,), jnp.float32)
        .at[owners * panel_count + panels]
        .add(values)
    )
    force = lax.psum_scatter(terms, "space", scatter_dimension=0, tiled=True)
    return (moved[None], phi[None], force[None])


def solution(mesh):
    return jax.shard_map(
        body,
        mesh=mesh,
        in_specs=(
            P("dir", None, "space", None, None),
            P("dir", None, "space", None),
            P("dir", "space", None),
            P("dir", "space"),
            P("dir", "space", None),
            P("dir", "space"),
            P("dir", "space"),
        ),
        out_specs=(
            P("dir", None, "space", None, None),
            P("dir", "space", None, None),
            P("dir", "space"),
        ),
        check_vma=False,
    )
```

profile of v0, /device:TPU:264, one launch (start us, length us, event | category | flops | bytes accessed | tf_op | source)
XLA Modules:
  0.0 643.1 jit_solution(17695690492703726004)
XLA Ops:
  8.0 62.6 %psum.7 = f32[3,8,512]{2,1,0:T(8,128)} all-reduce(f32[3,8,512]{2,1,0:T(8,128)S(1)} %select_bitcast_fusion), channel_id=1, replica_groups=mesh['dir'=16,'space'=32] {'dir'}, use_global_device_ids=true, to_apply=%region_0.1 | all-reduce | flops 12288 | bytes 98304 | tf_op jit(solution)/shard_map/psum | solution.py:31
  72.7 80.0 %all-gather.2.cloned.1.call-done = f32[3,256,512]{2,1,0:T(8,128)} async-done(((f32[3,8,512]{2,1,0:T(8,128)}), f32[3,256,512]{2,1,0:T(8,128)}) %all-gather.2.cloned.1.call-update) | async-done | bytes 1572880 | tf_op jit(solution)/shard_map/all_gather | solution.py:99
  152.7 32.7 %copy.14 = f32[3,256,512]{0,2,1:T(8,128)} copy(f32[3,256,512]{2,1,0:T(8,128)} %all-gather.2.cloned.1.call-done) | data formatting | bytes 3145728 | tf_op jit(solution)/shard_map/all_gather | solution.py:99
  185.4 60.0 %gather_fusion = f32[4096,3]{1,0:T(8,128)} fusion(f32[3,131072]{0,1:T(8,128)} %bitcast.3, s32[4096]{0:T(1024)S(1)} %broadcast_clamp_fusion), kind=kCustom, calls=%fused_computation | custom fusion | bytes 114688 | tf_op jit(solution)/shard_map/jit(_take)/gather | solution.py:101
  245.4 2.3 copy.15
  248.5 2.0 collective-permute-start.2
  250.6 7.1 %collective-permute-start.3 = (f32[3,2,16,512]{3,2,1,0:T(8,128)S(1)}, f32[3,2,16,512]{3,2,1,0:T(8,128)S(1)}, u32[]{:S(2)}, u32[]{:S(2)}) collective-permute-start(f32[3,2,16,512]{3,2,1,0:T(8,128)S(1)} %get-tuple-element.85), channel_id=1, source_target_pairs={{1,0},{2,1},{3,2},{4,3},{5,4},{6,5},{7,6},{8,7},{9,8},{10,9},{11,1... | collective-permute-start | bytes 589832 | tf_op jit(solution)/shard_map/ppermute | solution.py:22
  259.2 1.7 collective-permute-done.3
  264.6 227.4 %while.14 = (s32[]{:T(128)}, f32[8,16,512]{2,1,0:T(8,128)S(1)}, f32[8,16,512]{2,1,0:T(8,128)S(1)}, s32[]{:T(128)}, s32[]{:T(128)}) while((s32[]{:T(128)}, f32[8,16,512]{2,1,0:T(8,128)S(1)}, f32[8,16,512]{2,1,0:T(8,128)S(1)}, s32[]{:T(128)}, s32[]{:T(128)}) %tuple.48), condition=%wide.region_2.3_spmd.clone, body=%wide.region_1.2_spmd.clone.sunk | while | flops 2108699 | bytes 3515959 | solution.py:117
  264.7 2.1 collective-permute-start
  266.8 7.3 %collective-permute-start.1 = (f32[1,16,512]{2,1,0:T(8,128)S(1)}, f32[1,16,512]{2,1,0:T(8,128)S(1)}, u32[]{:S(2)}, u32[]{:S(2)}) collective-permute-start(f32[1,16,512]{2,1,0:T(8,128)S(1)} %get-tuple-element.112), channel_id=1, source_target_pairs={{1,0},{2,1},{3,2},{4,3},{5,4},{6,5},{7,6},{8,7},{9,8},{10,9},{11,1... | collective-permute-start | bytes 98312 | tf_op jit(solution)/shard_map/while/body/eval_jaxpr/ppermute | solution.py:22
  274.1 1.6 collective-permute-done.1
  276.2 1.9 collective-permute-start
  278.1 7.3 %collective-permute-start.1 = (f32[1,16,512]{2,1,0:T(8,128)S(1)}, f32[1,16,512]{2,1,0:T(8,128)S(1)}, u32[]{:S(2)}, u32[]{:S(2)}) collective-permute-start(f32[1,16,512]{2,1,0:T(8,128)S(1)} %get-tuple-element.112), channel_id=1, source_target_pairs={{1,0},{2,1},{3,2},{4,3},{5,4},{6,5},{7,6},{8,7},{9,8},{10,9},{11,1... | collective-permute-start | bytes 98312 | tf_op jit(solution)/shard_map/while/body/eval_jaxpr/ppermute | solution.py:22
  285.4 1.6 collective-permute-done.1
  287.6 1.9 collective-permute-start
  289.5 7.3 %collective-permute-start.1 = (f32[1,16,512]{2,1,0:T(8,128)S(1)}, f32[1,16,512]{2,1,0:T(8,128)S(1)}, u32[]{:S(2)}, u32[]{:S(2)}) collective-permute-start(f32[1,16,512]{2,1,0:T(8,128)S(1)} %get-tuple-element.112), channel_id=1, source_target_pairs={{1,0},{2,1},{3,2},{4,3},{5,4},{6,5},{7,6},{8,7},{9,8},{10,9},{11,1... | collective-permute-start | bytes 98312 | tf_op jit(solution)/shard_map/while/body/eval_jaxpr/ppermute | solution.py:22
  296.8 1.6 collective-permute-done.1
  298.9 1.9 collective-permute-start
  300.9 7.3 %collective-permute-start.1 = (f32[1,16,512]{2,1,0:T(8,128)S(1)}, f32[1,16,512]{2,1,0:T(8,128)S(1)}, u32[]{:S(2)}, u32[]{:S(2)}) collective-permute-start(f32[1,16,512]{2,1,0:T(8,128)S(1)} %get-tuple-element.112), channel_id=1, source_target_pairs={{1,0},{2,1},{3,2},{4,3},{5,4},{6,5},{7,6},{8,7},{9,8},{10,9},{11,1... | collective-permute-start | bytes 98312 | tf_op jit(solution)/shard_map/while/body/eval_jaxpr/ppermute | solution.py:22
  308.1 1.6 collective-permute-done.1
  310.3 1.9 collective-permute-start
  312.2 7.3 %collective-permute-start.1 = (f32[1,16,512]{2,1,0:T(8,128)S(1)}, f32[1,16,512]{2,1,0:T(8,128)S(1)}, u32[]{:S(2)}, u32[]{:S(2)}) collective-permute-start(f32[1,16,512]{2,1,0:T(8,128)S(1)} %get-tuple-element.112), channel_id=1, source_target_pairs={{1,0},{2,1},{3,2},{4,3},{5,4},{6,5},{7,6},{8,7},{9,8},{10,9},{11,1... | collective-permute-start | bytes 98312 | tf_op jit(solution)/shard_map/while/body/eval_jaxpr/ppermute | solution.py:22
  319.5 1.6 collective-permute-done.1
  321.6 1.9 collective-permute-start
  323.6 7.3 %collective-permute-start.1 = (f32[1,16,512]{2,1,0:T(8,128)S(1)}, f32[1,16,512]{2,1,0:T(8,128)S(1)}, u32[]{:S(2)}, u32[]{:S(2)}) collective-permute-start(f32[1,16,512]{2,1,0:T(8,128)S(1)} %get-tuple-element.112), channel_id=1, source_target_pairs={{1,0},{2,1},{3,2},{4,3},{5,4},{6,5},{7,6},{8,7},{9,8},{10,9},{11,1... | collective-permute-start | bytes 98312 | tf_op jit(solution)/shard_map/while/body/eval_jaxpr/ppermute | solution.py:22
  330.9 1.6 collective-permute-done.1
  333.0 1.9 collective-permute-start
  334.9 7.3 %collective-permute-start.1 = (f32[1,16,512]{2,1,0:T(8,128)S(1)}, f32[1,16,512]{2,1,0:T(8,128)S(1)}, u32[]{:S(2)}, u32[]{:S(2)}) collective-permute-start(f32[1,16,512]{2,1,0:T(8,128)S(1)} %get-tuple-element.112), channel_id=1, source_target_pairs={{1,0},{2,1},{3,2},{4,3},{5,4},{6,5},{7,6},{8,7},{9,8},{10,9},{11,1... | collective-permute-start | bytes 98312 | tf_op jit(solution)/shard_map/while/body/eval_jaxpr/ppermute | solution.py:22
  342.2 1.6 collective-permute-done.1
  344.4 1.9 collective-permute-start
  346.3 7.3 %collective-permute-start.1 = (f32[1,16,512]{2,1,0:T(8,128)S(1)}, f32[1,16,512]{2,1,0:T(8,128)S(1)}, u32[]{:S(2)}, u32[]{:S(2)}) collective-permute-start(f32[1,16,512]{2,1,0:T(8,128)S(1)} %get-tuple-element.112), channel_id=1, source_target_pairs={{1,0},{2,1},{3,2},{4,3},{5,4},{6,5},{7,6},{8,7},{9,8},{10,9},{11,1... | collective-permute-start | bytes 98312 | tf_op jit(solution)/shard_map/while/body/eval_jaxpr/ppermute | solution.py:22
  353.6 1.6 collective-permute-done.1
  355.7 1.9 collective-permute-start
  357.7 7.3 %collective-permute-start.1 = (f32[1,16,512]{2,1,0:T(8,128)S(1)}, f32[1,16,512]{2,1,0:T(8,128)S(1)}, u32[]{:S(2)}, u32[]{:S(2)}) collective-permute-start(f32[1,16,512]{2,1,0:T(8,128)S(1)} %get-tuple-element.112), channel_id=1, source_target_pairs={{1,0},{2,1},{3,2},{4,3},{5,4},{6,5},{7,6},{8,7},{9,8},{10,9},{11,1... | collective-permute-start | bytes 98312 | tf_op jit(solution)/shard_map/while/body/eval_jaxpr/ppermute | solution.py:22
  364.9 1.6 collective-permute-done.1
  367.1 1.9 collective-permute-start
  369.0 7.3 %collective-permute-start.1 = (f32[1,16,512]{2,1,0:T(8,128)S(1)}, f32[1,16,512]{2,1,0:T(8,128)S(1)}, u32[]{:S(2)}, u32[]{:S(2)}) collective-permute-start(f32[1,16,512]{2,1,0:T(8,128)S(1)} %get-tuple-element.112), channel_id=1, source_target_pairs={{1,0},{2,1},{3,2},{4,3},{5,4},{6,5},{7,6},{8,7},{9,8},{10,9},{11,1... | collective-permute-start | bytes 98312 | tf_op jit(solution)/shard_map/while/body/eval_jaxpr/ppermute | solution.py:22
  376.3 1.6 collective-permute-done.1
  378.4 1.9 collective-permute-start
  380.4 7.3 %collective-permute-start.1 = (f32[1,16,512]{2,1,0:T(8,128)S(1)}, f32[1,16,512]{2,1,0:T(8,128)S(1)}, u32[]{:S(2)}, u32[]{:S(2)}) collective-permute-start(f32[1,16,512]{2,1,0:T(8,128)S(1)} %get-tuple-element.112), channel_id=1, source_target_pairs={{1,0},{2,1},{3,2},{4,3},{5,4},{6,5},{7,6},{8,7},{9,8},{10,9},{11,1... | collective-permute-start | bytes 98312 | tf_op jit(solution)/shard_map/while/body/eval_jaxpr/ppermute | solution.py:22
  389.8 1.9 collective-permute-start
  391.7 7.3 %collective-permute-start.1 = (f32[1,16,512]{2,1,0:T(8,128)S(1)}, f32[1,16,512]{2,1,0:T(8,128)S(1)}, u32[]{:S(2)}, u32[]{:S(2)}) collective-permute-start(f32[1,16,512]{2,1,0:T(8,128)S(1)} %get-tuple-element.112), channel_id=1, source_target_pairs={{1,0},{2,1},{3,2},{4,3},{5,4},{6,5},{7,6},{8,7},{9,8},{10,9},{11,1... | collective-permute-start | bytes 98312 | tf_op jit(solution)/shard_map/while/body/eval_jaxpr/ppermute | solution.py:22
  401.2 1.9 collective-permute-start
  403.1 7.3 %collective-permute-start.1 = (f32[1,16,512]{2,1,0:T(8,128)S(1)}, f32[1,16,512]{2,1,0:T(8,128)S(1)}, u32[]{:S(2)}, u32[]{:S(2)}) collective-permute-start(f32[1,16,512]{2,1,0:T(8,128)S(1)} %get-tuple-element.112), channel_id=1, source_target_pairs={{1,0},{2,1},{3,2},{4,3},{5,4},{6,5},{7,6},{8,7},{9,8},{10,9},{11,1... | collective-permute-start | bytes 98312 | tf_op jit(solution)/shard_map/while/body/eval_jaxpr/ppermute | solution.py:22
  412.5 1.9 collective-permute-start
  414.5 7.3 %collective-permute-start.1 = (f32[1,16,512]{2,1,0:T(8,128)S(1)}, f32[1,16,512]{2,1,0:T(8,128)S(1)}, u32[]{:S(2)}, u32[]{:S(2)}) collective-permute-start(f32[1,16,512]{2,1,0:T(8,128)S(1)} %get-tuple-element.112), channel_id=1, source_target_pairs={{1,0},{2,1},{3,2},{4,3},{5,4},{6,5},{7,6},{8,7},{9,8},{10,9},{11,1... | collective-permute-start | bytes 98312 | tf_op jit(solution)/shard_map/while/body/eval_jaxpr/ppermute | solution.py:22
  423.9 1.9 collective-permute-start
  425.8 7.3 %collective-permute-start.1 = (f32[1,16,512]{2,1,0:T(8,128)S(1)}, f32[1,16,512]{2,1,0:T(8,128)S(1)}, u32[]{:S(2)}, u32[]{:S(2)}) collective-permute-start(f32[1,16,512]{2,1,0:T(8,128)S(1)} %get-tuple-element.112), channel_id=1, source_target_pairs={{1,0},{2,1},{3,2},{4,3},{5,4},{6,5},{7,6},{8,7},{9,8},{10,9},{11,1... | collective-permute-start | bytes 98312 | tf_op jit(solution)/shard_map/while/body/eval_jaxpr/ppermute | solution.py:22
  435.2 1.9 collective-permute-start
  437.2 7.3 %collective-permute-start.1 = (f32[1,16,512]{2,1,0:T(8,128)S(1)}, f32[1,16,512]{2,1,0:T(8,128)S(1)}, u32[]{:S(2)}, u32[]{:S(2)}) collective-permute-start(f32[1,16,512]{2,1,0:T(8,128)S(1)} %get-tuple-element.112), channel_id=1, source_target_pairs={{1,0},{2,1},{3,2},{4,3},{5,4},{6,5},{7,6},{8,7},{9,8},{10,9},{11,1... | collective-permute-start | bytes 98312 | tf_op jit(solution)/shard_map/while/body/eval_jaxpr/ppermute | solution.py:22
  446.6 1.9 collective-permute-start
  448.5 7.3 %collective-permute-start.1 = (f32[1,16,512]{2,1,0:T(8,128)S(1)}, f32[1,16,512]{2,1,0:T(8,128)S(1)}, u32[]{:S(2)}, u32[]{:S(2)}) collective-permute-start(f32[1,16,512]{2,1,0:T(8,128)S(1)} %get-tuple-element.112), channel_id=1, source_target_pairs={{1,0},{2,1},{3,2},{4,3},{5,4},{6,5},{7,6},{8,7},{9,8},{10,9},{11,1... | collective-permute-start | bytes 98312 | tf_op jit(solution)/shard_map/while/body/eval_jaxpr/ppermute | solution.py:22
  458.0 1.9 collective-permute-start
  459.9 7.3 %collective-permute-start.1 = (f32[1,16,512]{2,1,0:T(8,128)S(1)}, f32[1,16,512]{2,1,0:T(8,128)S(1)}, u32[]{:S(2)}, u32[]{:S(2)}) collective-permute-start(f32[1,16,512]{2,1,0:T(8,128)S(1)} %get-tuple-element.112), channel_id=1, source_target_pairs={{1,0},{2,1},{3,2},{4,3},{5,4},{6,5},{7,6},{8,7},{9,8},{10,9},{11,1... | collective-permute-start | bytes 98312 | tf_op jit(solution)/shard_map/while/body/eval_jaxpr/ppermute | solution.py:22
  469.3 1.9 collective-permute-start
  471.3 7.3 %collective-permute-start.1 = (f32[1,16,512]{2,1,0:T(8,128)S(1)}, f32[1,16,512]{2,1,0:T(8,128)S(1)}, u32[]{:S(2)}, u32[]{:S(2)}) collective-permute-start(f32[1,16,512]{2,1,0:T(8,128)S(1)} %get-tuple-element.112), channel_id=1, source_target_pairs={{1,0},{2,1},{3,2},{4,3},{5,4},{6,5},{7,6},{8,7},{9,8},{10,9},{11,1... | collective-permute-start | bytes 98312 | tf_op jit(solution)/shard_map/while/body/eval_jaxpr/ppermute | solution.py:22
  480.7 1.9 collective-permute-start
  482.6 7.3 %collective-permute-start.1 = (f32[1,16,512]{2,1,0:T(8,128)S(1)}, f32[1,16,512]{2,1,0:T(8,128)S(1)}, u32[]{:S(2)}, u32[]{:S(2)}) collective-permute-start(f32[1,16,512]{2,1,0:T(8,128)S(1)} %get-tuple-element.112), channel_id=1, source_target_pairs={{1,0},{2,1},{3,2},{4,3},{5,4},{6,5},{7,6},{8,7},{9,8},{10,9},{11,1... | collective-permute-start | bytes 98312 | tf_op jit(solution)/shard_map/while/body/eval_jaxpr/ppermute | solution.py:22
  492.0 2.1 collective-permute-start.4
  494.1 7.3 %collective-permute-start.5 = (f32[1,16,512]{2,1,0:T(8,128)S(1)}, f32[1,16,512]{2,1,0:T(8,128)S(1)}, u32[]{:S(2)}, u32[]{:S(2)}) collective-permute-start(f32[1,16,512]{2,1,0:T(8,128)S(1)} %get-tuple-element.89), channel_id=1, source_target_pairs={{1,0},{2,1},{3,2},{4,3},{5,4},{6,5},{7,6},{8,7},{9,8},{10,9},{11,1... | collective-permute-start | bytes 98312 | tf_op jit(solution)/shard_map/ppermute | solution.py:22
  501.4 1.7 gather_fusion.1
  503.2 1.9 scatter_custom_fusion
  505.1 129.0 %all-reduce.4 = f32[4096]{0:T(1024)S(1)} all-reduce(f32[4096]{0:T(1024)S(1)} %scatter_custom_fusion), channel_id=2, replica_groups=mesh['dir'=16,'space'=32] {'space'}, use_global_device_ids=true, to_apply=%region_4.5.clone | all-reduce | flops 4096 | bytes 32768
  (161 shorter events, 36.8 us)
Async XLA Ops:
  7.2 0.8 copy-start.3
  7.2 63.4 %copy-start.2 = (s32[1,8,512]{2,1,0:T(8,128)S(1)}, s32[1,8,512]{2,1,0:T(8,128)}, u32[]{:S(2)}) copy-start(s32[1,8,512]{2,1,0:T(8,128)} %param.13) | copy-start | bytes 49156
  7.2 65.4 %copy-start.7 = (s32[1,256]{1,0:T(1,128)S(1)}, s32[1,256]{1,0:T(1,128)}, u32[]{:S(2)}) copy-start(s32[1,256]{1,0:T(1,128)} %param.14) | copy-start | bytes 3076
  7.2 145.5 %all-gather.2.cloned.1.call-start = ((), (), s32[]{:S(2)}) async-start(), calls=%async_computation | async-start | bytes 1622016 | tf_op jit(solution)/shard_map/all_gather | solution.py:99
  245.4 2.4 copy-start.1
  245.4 12.3 %copy-start.4 = (s32[1,256]{1,0:T(1,128)S(1)}, s32[1,256]{1,0:T(1,128)}, u32[]{:S(2)}) copy-start(s32[1,256]{1,0:T(1,128)} %param.16) | copy-start | bytes 3076
  245.4 12.3 %copy-start.5 = (s32[1,256,1]{1,2,0:T(1,128)S(1)}, s32[1,256,1]{1,2,0:T(1,128)}, u32[]{:S(2)}) copy-start(s32[1,256,1]{1,2,0:T(1,128)} %param.15) | copy-start | bytes 3076
  248.5 10.7 %collective-permute-start.2 = (f32[3,2,16,512]{3,2,1,0:T(8,128)S(1)}, f32[3,2,16,512]{3,2,1,0:T(8,128)S(1)}, u32[]{:S(2)}, u32[]{:S(2)}) collective-permute-start(f32[3,2,16,512]{3,2,1,0:T(8,128)S(1)} %get-tuple-element.84), channel_id=1, source_target_pairs={{0,1},{1,2},{2,3},{3,4},{4,5},{5,6},{6,7},{7,8},{8,9},{9,10},{10,1... | collective-permute-start | bytes 589832 | tf_op jit(solution)/shard_map/ppermute | solution.py:20
  250.6 10.3 %collective-permute-start.3 = (f32[3,2,16,512]{3,2,1,0:T(8,128)S(1)}, f32[3,2,16,512]{3,2,1,0:T(8,128)S(1)}, u32[]{:S(2)}, u32[]{:S(2)}) collective-permute-start(f32[3,2,16,512]{3,2,1,0:T(8,128)S(1)} %get-tuple-element.85), channel_id=1, source_target_pairs={{1,0},{2,1},{3,2},{4,3},{5,4},{6,5},{7,6},{8,7},{9,8},{10,9},{11,1... | collective-permute-start | bytes 589832 | tf_op jit(solution)/shard_map/ppermute | solution.py:22
  264.7 9.4 %collective-permute-start = (f32[1,16,512]{2,1,0:T(8,128)S(1)}, f32[1,16,512]{2,1,0:T(8,128)S(1)}, u32[]{:S(2)}, u32[]{:S(2)}) collective-permute-start(f32[1,16,512]{2,1,0:T(8,128)S(1)} %get-tuple-element.111), channel_id=1, source_target_pairs={{0,1},{1,2},{2,3},{3,4},{4,5},{5,6},{6,7},{7,8},{8,9},{9,10},{10,1... | collective-permute-start | bytes 98312 | tf_op jit(solution)/shard_map/while/body/eval_jaxpr/ppermute | solution.py:20
  266.8 8.9 %collective-permute-start.1 = (f32[1,16,512]{2,1,0:T(8,128)S(1)}, f32[1,16,512]{2,1,0:T(8,128)S(1)}, u32[]{:S(2)}, u32[]{:S(2)}) collective-permute-start(f32[1,16,512]{2,1,0:T(8,128)S(1)} %get-tuple-element.112), channel_id=1, source_target_pairs={{1,0},{2,1},{3,2},{4,3},{5,4},{6,5},{7,6},{8,7},{9,8},{10,9},{11,1... | collective-permute-start | bytes 98312 | tf_op jit(solution)/shard_map/while/body/eval_jaxpr/ppermute | solution.py:22
  276.2 9.2 %collective-permute-start = (f32[1,16,512]{2,1,0:T(8,128)S(1)}, f32[1,16,512]{2,1,0:T(8,128)S(1)}, u32[]{:S(2)}, u32[]{:S(2)}) collective-permute-start(f32[1,16,512]{2,1,0:T(8,128)S(1)} %get-tuple-element.111), channel_id=1, source_target_pairs={{0,1},{1,2},{2,3},{3,4},{4,5},{5,6},{6,7},{7,8},{8,9},{9,10},{10,1... | collective-permute-start | bytes 98312 | tf_op jit(solution)/shard_map/while/body/eval_jaxpr/ppermute | solution.py:20
  278.1 8.8 %collective-permute-start.1 = (f32[1,16,512]{2,1,0:T(8,128)S(1)}, f32[1,16,512]{2,1,0:T(8,128)S(1)}, u32[]{:S(2)}, u32[]{:S(2)}) collective-permute-start(f32[1,16,512]{2,1,0:T(8,128)S(1)} %get-tuple-element.112), channel_id=1, source_target_pairs={{1,0},{2,1},{3,2},{4,3},{5,4},{6,5},{7,6},{8,7},{9,8},{10,9},{11,1... | collective-permute-start | bytes 98312 | tf_op jit(solution)/shard_map/while/body/eval_jaxpr/ppermute | solution.py:22
  287.6 9.2 %collective-permute-start = (f32[1,16,512]{2,1,0:T(8,128)S(1)}, f32[1,16,512]{2,1,0:T(8,128)S(1)}, u32[]{:S(2)}, u32[]{:S(2)}) collective-permute-start(f32[1,16,512]{2,1,0:T(8,128)S(1)} %get-tuple-element.111), channel_id=1, source_target_pairs={{0,1},{1,2},{2,3},{3,4},{4,5},{5,6},{6,7},{7,8},{8,9},{9,10},{10,1... | collective-permute-start | bytes 98312 | tf_op jit(solution)/shard_map/while/body/eval_jaxpr/ppermute | solution.py:20
  289.5 8.8 %collective-permute-start.1 = (f32[1,16,512]{2,1,0:T(8,128)S(1)}, f32[1,16,512]{2,1,0:T(8,128)S(1)}, u32[]{:S(2)}, u32[]{:S(2)}) collective-permute-start(f32[1,16,512]{2,1,0:T(8,128)S(1)} %get-tuple-element.112), channel_id=1, source_target_pairs={{1,0},{2,1},{3,2},{4,3},{5,4},{6,5},{7,6},{8,7},{9,8},{10,9},{11,1... | collective-permute-start | bytes 98312 | tf_op jit(solution)/shard_map/while/body/eval_jaxpr/ppermute | solution.py:22
  298.9 9.2 %collective-permute-start = (f32[1,16,512]{2,1,0:T(8,128)S(1)}, f32[1,16,512]{2,1,0:T(8,128)S(1)}, u32[]{:S(2)}, u32[]{:S(2)}) collective-permute-start(f32[1,16,512]{2,1,0:T(8,128)S(1)} %get-tuple-element.111), channel_id=1, source_target_pairs={{0,1},{1,2},{2,3},{3,4},{4,5},{5,6},{6,7},{7,8},{8,9},{9,10},{10,1... | collective-permute-start | bytes 98312 | tf_op jit(solution)/shard_map/while/body/eval_jaxpr/ppermute | solution.py:20
  300.9 8.8 %collective-permute-start.1 = (f32[1,16,512]{2,1,0:T(8,128)S(1)}, f32[1,16,512]{2,1,0:T(8,128)S(1)}, u32[]{:S(2)}, u32[]{:S(2)}) collective-permute-start(f32[1,16,512]{2,1,0:T(8,128)S(1)} %get-tuple-element.112), channel_id=1, source_target_pairs={{1,0},{2,1},{3,2},{4,3},{5,4},{6,5},{7,6},{8,7},{9,8},{10,9},{11,1... | collective-permute-start | bytes 98312 | tf_op jit(solution)/shard_map/while/body/eval_jaxpr/ppermute | solution.py:22
  310.3 9.2 %collective-permute-start = (f32[1,16,512]{2,1,0:T(8,128)S(1)}, f32[1,16,512]{2,1,0:T(8,128)S(1)}, u32[]{:S(2)}, u32[]{:S(2)}) collective-permute-start(f32[1,16,512]{2,1,0:T(8,128)S(1)} %get-tuple-element.111), channel_id=1, source_target_pairs={{0,1},{1,2},{2,3},{3,4},{4,5},{5,6},{6,7},{7,8},{8,9},{9,10},{10,1... | collective-permute-start | bytes 98312 | tf_op jit(solution)/shard_map/while/body/eval_jaxpr/ppermute | solution.py:20
  312.2 8.8 %collective-permute-start.1 = (f32[1,16,512]{2,1,0:T(8,128)S(1)}, f32[1,16,512]{2,1,0:T(8,128)S(1)}, u32[]{:S(2)}, u32[]{:S(2)}) collective-permute-start(f32[1,16,512]{2,1,0:T(8,128)S(1)} %get-tuple-element.112), channel_id=1, source_target_pairs={{1,0},{2,1},{3,2},{4,3},{5,4},{6,5},{7,6},{8,7},{9,8},{10,9},{11,1... | collective-permute-start | bytes 98312 | tf_op jit(solution)/shard_map/while/body/eval_jaxpr/ppermute | solution.py:22
  321.6 9.2 %collective-permute-start = (f32[1,16,512]{2,1,0:T(8,128)S(1)}, f32[1,16,512]{2,1,0:T(8,128)S(1)}, u32[]{:S(2)}, u32[]{:S(2)}) collective-permute-start(f32[1,16,512]{2,1,0:T(8,128)S(1)} %get-tuple-element.111), channel_id=1, source_target_pairs={{0,1},{1,2},{2,3},{3,4},{4,5},{5,6},{6,7},{7,8},{8,9},{9,10},{10,1... | collective-permute-start | bytes 98312 | tf_op jit(solution)/shard_map/while/body/eval_jaxpr/ppermute | solution.py:20
  323.6 8.8 %collective-permute-start.1 = (f32[1,16,512]{2,1,0:T(8,128)S(1)}, f32[1,16,512]{2,1,0:T(8,128)S(1)}, u32[]{:S(2)}, u32[]{:S(2)}) collective-permute-start(f32[1,16,512]{2,1,0:T(8,128)S(1)} %get-tuple-element.112), channel_id=1, source_target_pairs={{1,0},{2,1},{3,2},{4,3},{5,4},{6,5},{7,6},{8,7},{9,8},{10,9},{11,1... | collective-permute-start | bytes 98312 | tf_op jit(solution)/shard_map/while/body/eval_jaxpr/ppermute | solution.py:22
  333.0 9.2 %collective-permute-start = (f32[1,16,512]{2,1,0:T(8,128)S(1)}, f32[1,16,512]{2,1,0:T(8,128)S(1)}, u32[]{:S(2)}, u32[]{:S(2)}) collective-permute-start(f32[1,16,512]{2,1,0:T(8,128)S(1)} %get-tuple-element.111), channel_id=1, source_target_pairs={{0,1},{1,2},{2,3},{3,4},{4,5},{5,6},{6,7},{7,8},{8,9},{9,10},{10,1... | collective-permute-start | bytes 98312 | tf_op jit(solution)/shard_map/while/body/eval_jaxpr/ppermute | solution.py:20
  334.9 8.8 %collective-permute-start.1 = (f32[1,16,512]{2,1,0:T(8,128)S(1)}, f32[1,16,512]{2,1,0:T(8,128)S(1)}, u32[]{:S(2)}, u32[]{:S(2)}) collective-permute-start(f32[1,16,512]{2,1,0:T(8,128)S(1)} %get-tuple-element.112), channel_id=1, source_target_pairs={{1,0},{2,1},{3,2},{4,3},{5,4},{6,5},{7,6},{8,7},{9,8},{10,9},{11,1... | collective-permute-start | bytes 98312 | tf_op jit(solution)/shard_map/while/body/eval_jaxpr/ppermute | solution.py:22
  344.4 9.2 %collective-permute-start = (f32[1,16,512]{2,1,0:T(8,128)S(1)}, f32[1,16,512]{2,1,0:T(8,128)S(1)}, u32[]{:S(2)}, u32[]{:S(2)}) collective-permute-start(f32[1,16,512]{2,1,0:T(8,128)S(1)} %get-tuple-element.111), channel_id=1, source_target_pairs={{0,1},{1,2},{2,3},{3,4},{4,5},{5,6},{6,7},{7,8},{8,9},{9,10},{10,1... | collective-permute-start | bytes 98312 | tf_op jit(solution)/shard_map/while/body/eval_jaxpr/ppermute | solution.py:20
  346.3 8.8 %collective-permute-start.1 = (f32[1,16,512]{2,1,0:T(8,128)S(1)}, f32[1,16,512]{2,1,0:T(8,128)S(1)}, u32[]{:S(2)}, u32[]{:S(2)}) collective-permute-start(f32[1,16,512]{2,1,0:T(8,128)S(1)} %get-tuple-element.112), channel_id=1, source_target_pairs={{1,0},{2,1},{3,2},{4,3},{5,4},{6,5},{7,6},{8,7},{9,8},{10,9},{11,1... | collective-permute-start | bytes 98312 | tf_op jit(solution)/shard_map/while/body/eval_jaxpr/ppermute | solution.py:22
  355.7 9.2 %collective-permute-start = (f32[1,16,512]{2,1,0:T(8,128)S(1)}, f32[1,16,512]{2,1,0:T(8,128)S(1)}, u32[]{:S(2)}, u32[]{:S(2)}) collective-permute-start(f32[1,16,512]{2,1,0:T(8,128)S(1)} %get-tuple-element.111), channel_id=1, source_target_pairs={{0,1},{1,2},{2,3},{3,4},{4,5},{5,6},{6,7},{7,8},{8,9},{9,10},{10,1... | collective-permute-start | bytes 98312 | tf_op jit(solution)/shard_map/while/body/eval_jaxpr/ppermute | solution.py:20
  357.7 8.8 %collective-permute-start.1 = (f32[1,16,512]{2,1,0:T(8,128)S(1)}, f32[1,16,512]{2,1,0:T(8,128)S(1)}, u32[]{:S(2)}, u32[]{:S(2)}) collective-permute-start(f32[1,16,512]{2,1,0:T(8,128)S(1)} %get-tuple-element.112), channel_id=1, source_target_pairs={{1,0},{2,1},{3,2},{4,3},{5,4},{6,5},{7,6},{8,7},{9,8},{10,9},{11,1... | collective-permute-start | bytes 98312 | tf_op jit(solution)/shard_map/while/body/eval_jaxpr/ppermute | solution.py:22
  367.1 9.2 %collective-permute-start = (f32[1,16,512]{2,1,0:T(8,128)S(1)}, f32[1,16,512]{2,1,0:T(8,128)S(1)}, u32[]{:S(2)}, u32[]{:S(2)}) collective-permute-start(f32[1,16,512]{2,1,0:T(8,128)S(1)} %get-tuple-element.111), channel_id=1, source_target_pairs={{0,1},{1,2},{2,3},{3,4},{4,5},{5,6},{6,7},{7,8},{8,9},{9,10},{10,1... | collective-permute-start | bytes 98312 | tf_op jit(solution)/shard_map/while/body/eval_jaxpr/ppermute | solution.py:20
  369.0 8.8 %collective-permute-start.1 = (f32[1,16,512]{2,1,0:T(8,128)S(1)}, f32[1,16,512]{2,1,0:T(8,128)S(1)}, u32[]{:S(2)}, u32[]{:S(2)}) collective-permute-start(f32[1,16,512]{2,1,0:T(8,128)S(1)} %get-tuple-element.112), channel_id=1, source_target_pairs={{1,0},{2,1},{3,2},{4,3},{5,4},{6,5},{7,6},{8,7},{9,8},{10,9},{11,1... | collective-permute-start | bytes 98312 | tf_op jit(solution)/shard_map/while/body/eval_jaxpr/ppermute | solution.py:22
  378.4 9.2 %collective-permute-start = (f32[1,16,512]{2,1,0:T(8,128)S(1)}, f32[1,16,512]{2,1,0:T(8,128)S(1)}, u32[]{:S(2)}, u32[]{:S(2)}) collective-permute-start(f32[1,16,512]{2,1,0:T(8,128)S(1)} %get-tuple-element.111), channel_id=1, source_target_pairs={{0,1},{1,2},{2,3},{3,4},{4,5},{5,6},{6,7},{7,8},{8,9},{9,10},{10,1... | collective-permute-start | bytes 98312 | tf_op jit(solution)/shard_map/while/body/eval_jaxpr/ppermute | solution.py:20
  380.4 8.8 %collective-permute-start.1 = (f32[1,16,512]{2,1,0:T(8,128)S(1)}, f32[1,16,512]{2,1,0:T(8,128)S(1)}, u32[]{:S(2)}, u32[]{:S(2)}) collective-permute-start(f32[1,16,512]{2,1,0:T(8,128)S(1)} %get-tuple-element.112), channel_id=1, source_target_pairs={{1,0},{2,1},{3,2},{4,3},{5,4},{6,5},{7,6},{8,7},{9,8},{10,9},{11,1... | collective-permute-start | bytes 98312 | tf_op jit(solution)/shard_map/while/body/eval_jaxpr/ppermute | solution.py:22
  389.8 9.2 %collective-permute-start = (f32[1,16,512]{2,1,0:T(8,128)S(1)}, f32[1,16,512]{2,1,0:T(8,128)S(1)}, u32[]{:S(2)}, u32[]{:S(2)}) collective-permute-start(f32[1,16,512]{2,1,0:T(8,128)S(1)} %get-tuple-element.111), channel_id=1, source_target_pairs={{0,1},{1,2},{2,3},{3,4},{4,5},{5,6},{6,7},{7,8},{8,9},{9,10},{10,1... | collective-permute-start | bytes 98312 | tf_op jit(solution)/shard_map/while/body/eval_jaxpr/ppermute | solution.py:20
  391.7 8.8 %collective-permute-start.1 = (f32[1,16,512]{2,1,0:T(8,128)S(1)}, f32[1,16,512]{2,1,0:T(8,128)S(1)}, u32[]{:S(2)}, u32[]{:S(2)}) collective-permute-start(f32[1,16,512]{2,1,0:T(8,128)S(1)} %get-tuple-element.112), channel_id=1, source_target_pairs={{1,0},{2,1},{3,2},{4,3},{5,4},{6,5},{7,6},{8,7},{9,8},{10,9},{11,1... | collective-permute-start | bytes 98312 | tf_op jit(solution)/shard_map/while/body/eval_jaxpr/ppermute | solution.py:22
  401.2 9.2 %collective-permute-start = (f32[1,16,512]{2,1,0:T(8,128)S(1)}, f32[1,16,512]{2,1,0:T(8,128)S(1)}, u32[]{:S(2)}, u32[]{:S(2)}) collective-permute-start(f32[1,16,512]{2,1,0:T(8,128)S(1)} %get-tuple-element.111), channel_id=1, source_target_pairs={{0,1},{1,2},{2,3},{3,4},{4,5},{5,6},{6,7},{7,8},{8,9},{9,10},{10,1... | collective-permute-start | bytes 98312 | tf_op jit(solution)/shard_map/while/body/eval_jaxpr/ppermute | solution.py:20
  403.1 8.8 %collective-permute-start.1 = (f32[1,16,512]{2,1,0:T(8,128)S(1)}, f32[1,16,512]{2,1,0:T(8,128)S(1)}, u32[]{:S(2)}, u32[]{:S(2)}) collective-permute-start(f32[1,16,512]{2,1,0:T(8,128)S(1)} %get-tuple-element.112), channel_id=1, source_target_pairs={{1,0},{2,1},{3,2},{4,3},{5,4},{6,5},{7,6},{8,7},{9,8},{10,9},{11,1... | collective-permute-start | bytes 98312 | tf_op jit(solution)/shard_map/while/body/eval_jaxpr/ppermute | solution.py:22
  412.5 9.2 %collective-permute-start = (f32[1,16,512]{2,1,0:T(8,128)S(1)}, f32[1,16,512]{2,1,0:T(8,128)S(1)}, u32[]{:S(2)}, u32[]{:S(2)}) collective-permute-start(f32[1,16,512]{2,1,0:T(8,128)S(1)} %get-tuple-element.111), channel_id=1, source_target_pairs={{0,1},{1,2},{2,3},{3,4},{4,5},{5,6},{6,7},{7,8},{8,9},{9,10},{10,1... | collective-permute-start | bytes 98312 | tf_op jit(solution)/shard_map/while/body/eval_jaxpr/ppermute | solution.py:20
  414.5 8.8 %collective-permute-start.1 = (f32[1,16,512]{2,1,0:T(8,128)S(1)}, f32[1,16,512]{2,1,0:T(8,128)S(1)}, u32[]{:S(2)}, u32[]{:S(2)}) collective-permute-start(f32[1,16,512]{2,1,0:T(8,128)S(1)} %get-tuple-element.112), channel_id=1, source_target_pairs={{1,0},{2,1},{3,2},{4,3},{5,4},{6,5},{7,6},{8,7},{9,8},{10,9},{11,1... | collective-permute-start | bytes 98312 | tf_op jit(solution)/shard_map/while/body/eval_jaxpr/ppermute | solution.py:22
  423.9 9.2 %collective-permute-start = (f32[1,16,512]{2,1,0:T(8,128)S(1)}, f32[1,16,512]{2,1,0:T(8,128)S(1)}, u32[]{:S(2)}, u32[]{:S(2)}) collective-permute-start(f32[1,16,512]{2,1,0:T(8,128)S(1)} %get-tuple-element.111), channel_id=1, source_target_pairs={{0,1},{1,2},{2,3},{3,4},{4,5},{5,6},{6,7},{7,8},{8,9},{9,10},{10,1... | collective-permute-start | bytes 98312 | tf_op jit(solution)/shard_map/while/body/eval_jaxpr/ppermute | solution.py:20
  425.8 8.8 %collective-permute-start.1 = (f32[1,16,512]{2,1,0:T(8,128)S(1)}, f32[1,16,512]{2,1,0:T(8,128)S(1)}, u32[]{:S(2)}, u32[]{:S(2)}) collective-permute-start(f32[1,16,512]{2,1,0:T(8,128)S(1)} %get-tuple-element.112), channel_id=1, source_target_pairs={{1,0},{2,1},{3,2},{4,3},{5,4},{6,5},{7,6},{8,7},{9,8},{10,9},{11,1... | collective-permute-start | bytes 98312 | tf_op jit(solution)/shard_map/while/body/eval_jaxpr/ppermute | solution.py:22
  435.2 9.2 %collective-permute-start = (f32[1,16,512]{2,1,0:T(8,128)S(1)}, f32[1,16,512]{2,1,0:T(8,128)S(1)}, u32[]{:S(2)}, u32[]{:S(2)}) collective-permute-start(f32[1,16,512]{2,1,0:T(8,128)S(1)} %get-tuple-element.111), channel_id=1, source_target_pairs={{0,1},{1,2},{2,3},{3,4},{4,5},{5,6},{6,7},{7,8},{8,9},{9,10},{10,1... | collective-permute-start | bytes 98312 | tf_op jit(solution)/shard_map/while/body/eval_jaxpr/ppermute | solution.py:20
  437.2 8.8 %collective-permute-start.1 = (f32[1,16,512]{2,1,0:T(8,128)S(1)}, f32[1,16,512]{2,1,0:T(8,128)S(1)}, u32[]{:S(2)}, u32[]{:S(2)}) collective-permute-start(f32[1,16,512]{2,1,0:T(8,128)S(1)} %get-tuple-element.112), channel_id=1, source_target_pairs={{1,0},{2,1},{3,2},{4,3},{5,4},{6,5},{7,6},{8,7},{9,8},{10,9},{11,1... | collective-permute-start | bytes 98312 | tf_op jit(solution)/shard_map/while/body/eval_jaxpr/ppermute | solution.py:22
  446.6 9.2 %collective-permute-start = (f32[1,16,512]{2,1,0:T(8,128)S(1)}, f32[1,16,512]{2,1,0:T(8,128)S(1)}, u32[]{:S(2)}, u32[]{:S(2)}) collective-permute-start(f32[1,16,512]{2,1,0:T(8,128)S(1)} %get-tuple-element.111), channel_id=1, source_target_pairs={{0,1},{1,2},{2,3},{3,4},{4,5},{5,6},{6,7},{7,8},{8,9},{9,10},{10,1... | collective-permute-start | bytes 98312 | tf_op jit(solution)/shard_map/while/body/eval_jaxpr/ppermute | solution.py:20
  448.5 8.8 %collective-permute-start.1 = (f32[1,16,512]{2,1,0:T(8,128)S(1)}, f32[1,16,512]{2,1,0:T(8,128)S(1)}, u32[]{:S(2)}, u32[]{:S(2)}) collective-permute-start(f32[1,16,512]{2,1,0:T(8,128)S(1)} %get-tuple-element.112), channel_id=1, source_target_pairs={{1,0},{2,1},{3,2},{4,3},{5,4},{6,5},{7,6},{8,7},{9,8},{10,9},{11,1... | collective-permute-start | bytes 98312 | tf_op jit(solution)/shard_map/while/body/eval_jaxpr/ppermute | solution.py:22
  458.0 9.2 %collective-permute-start = (f32[1,16,512]{2,1,0:T(8,128)S(1)}, f32[1,16,512]{2,1,0:T(8,128)S(1)}, u32[]{:S(2)}, u32[]{:S(2)}) collective-permute-start(f32[1,16,512]{2,1,0:T(8,128)S(1)} %get-tuple-element.111), channel_id=1, source_target_pairs={{0,1},{1,2},{2,3},{3,4},{4,5},{5,6},{6,7},{7,8},{8,9},{9,10},{10,1... | collective-permute-start | bytes 98312 | tf_op jit(solution)/shard_map/while/body/eval_jaxpr/ppermute | solution.py:20
  459.9 8.8 %collective-permute-start.1 = (f32[1,16,512]{2,1,0:T(8,128)S(1)}, f32[1,16,512]{2,1,0:T(8,128)S(1)}, u32[]{:S(2)}, u32[]{:S(2)}) collective-permute-start(f32[1,16,512]{2,1,0:T(8,128)S(1)} %get-tuple-element.112), channel_id=1, source_target_pairs={{1,0},{2,1},{3,2},{4,3},{5,4},{6,5},{7,6},{8,7},{9,8},{10,9},{11,1... | collective-permute-start | bytes 98312 | tf_op jit(solution)/shard_map/while/body/eval_jaxpr/ppermute | solution.py:22
  469.3 9.2 %collective-permute-start = (f32[1,16,512]{2,1,0:T(8,128)S(1)}, f32[1,16,512]{2,1,0:T(8,128)S(1)}, u32[]{:S(2)}, u32[]{:S(2)}) collective-permute-start(f32[1,16,512]{2,1,0:T(8,128)S(1)} %get-tuple-element.111), channel_id=1, source_target_pairs={{0,1},{1,2},{2,3},{3,4},{4,5},{5,6},{6,7},{7,8},{8,9},{9,10},{10,1... | collective-permute-start | bytes 98312 | tf_op jit(solution)/shard_map/while/body/eval_jaxpr/ppermute | solution.py:20
  471.3 8.8 %collective-permute-start.1 = (f32[1,16,512]{2,1,0:T(8,128)S(1)}, f32[1,16,512]{2,1,0:T(8,128)S(1)}, u32[]{:S(2)}, u32[]{:S(2)}) collective-permute-start(f32[1,16,512]{2,1,0:T(8,128)S(1)} %get-tuple-element.112), channel_id=1, source_target_pairs={{1,0},{2,1},{3,2},{4,3},{5,4},{6,5},{7,6},{8,7},{9,8},{10,9},{11,1... | collective-permute-start | bytes 98312 | tf_op jit(solution)/shard_map/while/body/eval_jaxpr/ppermute | solution.py:22
  480.7 9.2 %collective-permute-start = (f32[1,16,512]{2,1,0:T(8,128)S(1)}, f32[1,16,512]{2,1,0:T(8,128)S(1)}, u32[]{:S(2)}, u32[]{:S(2)}) collective-permute-start(f32[1,16,512]{2,1,0:T(8,128)S(1)} %get-tuple-element.111), channel_id=1, source_target_pairs={{0,1},{1,2},{2,3},{3,4},{4,5},{5,6},{6,7},{7,8},{8,9},{9,10},{10,1... | collective-permute-start | bytes 98312 | tf_op jit(solution)/shard_map/while/body/eval_jaxpr/ppermute | solution.py:20
  482.6 8.8 %collective-permute-start.1 = (f32[1,16,512]{2,1,0:T(8,128)S(1)}, f32[1,16,512]{2,1,0:T(8,128)S(1)}, u32[]{:S(2)}, u32[]{:S(2)}) collective-permute-start(f32[1,16,512]{2,1,0:T(8,128)S(1)} %get-tuple-element.112), channel_id=1, source_target_pairs={{1,0},{2,1},{3,2},{4,3},{5,4},{6,5},{7,6},{8,7},{9,8},{10,9},{11,1... | collective-permute-start | bytes 98312 | tf_op jit(solution)/shard_map/while/body/eval_jaxpr/ppermute | solution.py:22
  492.0 143.2 %copy-start = (f32[8,16,512]{2,1,0:T(8,128)}, f32[8,16,512]{2,1,0:T(8,128)S(1)}, u32[]{:S(2)}) copy-start(f32[8,16,512]{2,1,0:T(8,128)S(1)} %get-tuple-element.56) | copy-start | bytes 786436
  492.0 11.2 %copy-start.6 = (f32[1,256]{1,0:T(1,128)S(1)}, f32[1,256]{1,0:T(1,128)}, u32[]{:S(2)}) copy-start(f32[1,256]{1,0:T(1,128)} %param.17) | copy-start | bytes 3076
  492.0 142.7 %collective-permute-start.4 = (f32[1,16,512]{2,1,0:T(8,128)S(1)}, f32[1,16,512]{2,1,0:T(8,128)S(1)}, u32[]{:S(2)}, u32[]{:S(2)}) collective-permute-start(f32[1,16,512]{2,1,0:T(8,128)S(1)} %get-tuple-element.88), channel_id=1, source_target_pairs={{0,1},{1,2},{2,3},{3,4},{4,5},{5,6},{6,7},{7,8},{8,9},{9,10},{10,1... | collective-permute-start | bytes 98312 | tf_op jit(solution)/shard_map/ppermute | solution.py:20
  494.1 140.6 %collective-permute-start.5 = (f32[1,16,512]{2,1,0:T(8,128)S(1)}, f32[1,16,512]{2,1,0:T(8,128)S(1)}, u32[]{:S(2)}, u32[]{:S(2)}) collective-permute-start(f32[1,16,512]{2,1,0:T(8,128)S(1)} %get-tuple-element.89), channel_id=1, source_target_pairs={{1,0},{2,1},{3,2},{4,3},{5,4},{6,5},{7,6},{8,7},{9,8},{10,9},{11,1... | collective-permute-start | bytes 98312 | tf_op jit(solution)/shard_map/ppermute | solution.py:22
Sparse Core Ops, SparseCore 0:
  70.7 81.9 all-gather.1
where the time goes:
time: 646 us; the launch traced here: 643 us
  starting transfers between devices  202 us (31%)
  blocking collectives  192 us (30%)
  waiting for transfers between devices  115 us (18%)
  local copies, waits for them, and re-layouts  102 us (16%)
  other arithmetic  16.1 us (2%)
  between operations  15 us (2%)
    ppermute x22, starting transfers between devices, extended_2(): lax.ppermute(head, axis, [((i + 1) % count, i) for i in range(ends)])  160 us
    unnamed x1, blocking collectives  129 us
    all_gather x1, waiting for transfers between devices, body(): plane = lax.all_gather(plane_piece[0], 'space', axis=1, tiled=True)  80 us
    psum x1, blocking collectives, spread(): return lax.psum(block, axis)  62.6 us
    gather x2, local copies, waits for them, and re-layouts, body(): jnp.take(flat_plane, rot_map[0].reshape(-1), axis=1)  62.2 us
    ppermute x22, starting transfers between devices, extended_2(): lax.ppermute(tail, axis, [(i, (i + 1) % count) for i in range(ends)])  42.7 us
    ppermute x22, waiting for transfers between devices, extended_2(): lax.ppermute(head, axis, [((i + 1) % count, i) for i in range(ends)])  33 us
    all_gather x1, local copies, waits for them, and re-layouts, body(): plane = lax.all_gather(plane_piece[0], 'space', axis=1, tiled=True)  32.7 us
  transfers between devices with their start and end apart: 45, of which 23 were waited for; matrix products, arithmetic and copies ran while one was open for 1% of the time, Pallas kernels for 0%

commit v1 on v0

--- a/solution.py
+++ b/solution.py
@@ -28,7 +28,7 @@
 
 def spread(block, axis, holder):
     block = jnp.where(lax.axis_index(axis) == holder, block, jnp.zeros_like(block))
-    return lax.psum(block, axis)
+    return jnp.sum(lax.all_gather(block, axis), 0)
 
 
 def pad_edges(field):

time: 646 us -> 620 us (0.960)
  blocking collectives: 192 us -> 165 us
    psum x1 -> x0, blocking collectives: 62.6 us -> none  [spread(): return lax.psum(block, axis)]
    all_gather x0 -> x1, blocking collectives: none -> 36.4 us  [spread(): return jnp.sum(lax.all_gather(block, axis), 0)]
where the time goes in v1:
time: 620 us; the launch traced here: 617 us
  starting transfers between devices  202 us (33%)
  blocking collectives  165 us (27%)
  waiting for transfers between devices  114 us (18%)
  local copies, waits for them, and re-layouts  102 us (16%)
  other arithmetic  16.8 us (3%)
  between operations  15 us (2%)
    ppermute x22, starting transfers between devices, extended_2(): lax.ppermute(head, axis, [((i + 1) % count, i) for i in range(ends)])  160 us
    unnamed x1, blocking collectives  129 us
    all_gather x1, waiting for transfers between devices, body(): plane = lax.all_gather(plane_piece[0], 'space', axis=1, tiled=True)  79.9 us
    gather x2, local copies, waits for them, and re-layouts, body(): jnp.take(flat_plane, rot_map[0].reshape(-1), axis=1)  62.2 us
    ppermute x22, starting transfers between devices, extended_2(): lax.ppermute(tail, axis, [(i, (i + 1) % count) for i in range(ends)])  42.7 us
    all_gather x1, blocking collectives, spread(): return jnp.sum(lax.all_gather(block, axis), 0)  36.4 us
    ppermute x22, waiting for transfers between devices, extended_2(): lax.ppermute(head, axis, [((i + 1) % count, i) for i in range(ends)])  33 us
    all_gather x1, local copies, waits for them, and re-layouts, body(): plane = lax.all_gather(plane_piece[0], 'space', axis=1, tiled=True)  32.7 us
  transfers between devices with their start and end apart: 45, of which 23 were waited for; matrix products, arithmetic and copies ran while one was open for 1% of the time, Pallas kernels for 0%

profile of v1, /device:TPU:264, one launch (start us, length us, event | category | flops | bytes accessed | tf_op | source)
XLA Modules:
  0.0 617.5 jit_solution(7491330444390694731)
XLA Ops:
  8.0 36.4 %all-gather = f32[16,3,8,512]{3,2,1,0:T(8,128)S(1)} all-gather(f32[1,3,8,512]{3,2,1,0:T(8,128)S(1)} %broadcast_select_fusion.2), channel_id=2, replica_groups=mesh['dir'=16,'space'=32] {'dir'}, dimensions={0}, use_global_device_ids=true | all-gather | bytes 835584 | tf_op jit(solution)/shard_map/all_gather | solution.py:31
  47.1 79.9 %all-gather.3.cloned.1.call-done = f32[3,256,512]{2,1,0:T(8,128)} async-done(((f32[3,8,512]{2,1,0:T(8,128)}), f32[3,256,512]{2,1,0:T(8,128)}) %all-gather.3.cloned.1.call-update) | async-done | bytes 1572880 | tf_op jit(solution)/shard_map/all_gather | solution.py:99
  127.0 32.7 %copy.12 = f32[3,256,512]{0,2,1:T(8,128)} copy(f32[3,256,512]{2,1,0:T(8,128)} %all-gather.3.cloned.1.call-done) | data formatting | bytes 3145728 | tf_op jit(solution)/shard_map/all_gather | solution.py:99
  159.8 60.0 %gather_fusion = f32[4096,3]{1,0:T(8,128)} fusion(f32[3,131072]{0,1:T(8,128)} %bitcast.2, s32[4096]{0:T(1024)S(1)} %broadcast_clamp_fusion), kind=kCustom, calls=%fused_computation | custom fusion | bytes 114688 | tf_op jit(solution)/shard_map/jit(_take)/gather | solution.py:101
  219.8 2.3 copy.13
  222.9 2.0 collective-permute-start.2
  224.9 7.1 %collective-permute-start.3 = (f32[3,2,16,512]{3,2,1,0:T(8,128)S(1)}, f32[3,2,16,512]{3,2,1,0:T(8,128)S(1)}, u32[]{:S(2)}, u32[]{:S(2)}) collective-permute-start(f32[3,2,16,512]{3,2,1,0:T(8,128)S(1)} %get-tuple-element.85), channel_id=1, source_target_pairs={{1,0},{2,1},{3,2},{4,3},{5,4},{6,5},{7,6},{8,7},{9,8},{10,9},{11,1... | collective-permute-start | bytes 589832 | tf_op jit(solution)/shard_map/ppermute | solution.py:22
  233.6 1.7 collective-permute-done.3
  239.0 227.4 %while.14 = (s32[]{:T(128)}, f32[8,16,512]{2,1,0:T(8,128)S(1)}, f32[8,16,512]{2,1,0:T(8,128)S(1)}, s32[]{:T(128)}, s32[]{:T(128)}) while((s32[]{:T(128)}, f32[8,16,512]{2,1,0:T(8,128)S(1)}, f32[8,16,512]{2,1,0:T(8,128)S(1)}, s32[]{:T(128)}, s32[]{:T(128)}) %tuple.48), condition=%wide.region_2.3_spmd.clone, body=%wide.region_1.2_spmd.clone.sunk | while | flops 2108699 | bytes 3515959 | solution.py:117
  239.0 2.1 collective-permute-start
  241.1 7.3 %collective-permute-start.1 = (f32[1,16,512]{2,1,0:T(8,128)S(1)}, f32[1,16,512]{2,1,0:T(8,128)S(1)}, u32[]{:S(2)}, u32[]{:S(2)}) collective-permute-start(f32[1,16,512]{2,1,0:T(8,128)S(1)} %get-tuple-element.112), channel_id=1, source_target_pairs={{1,0},{2,1},{3,2},{4,3},{5,4},{6,5},{7,6},{8,7},{9,8},{10,9},{11,1... | collective-permute-start | bytes 98312 | tf_op jit(solution)/shard_map/while/body/eval_jaxpr/ppermute | solution.py:22
  248.4 1.6 collective-permute-done.1
  250.5 1.9 collective-permute-start
  252.5 7.3 %collective-permute-start.1 = (f32[1,16,512]{2,1,0:T(8,128)S(1)}, f32[1,16,512]{2,1,0:T(8,128)S(1)}, u32[]{:S(2)}, u32[]{:S(2)}) collective-permute-start(f32[1,16,512]{2,1,0:T(8,128)S(1)} %get-tuple-element.112), channel_id=1, source_target_pairs={{1,0},{2,1},{3,2},{4,3},{5,4},{6,5},{7,6},{8,7},{9,8},{10,9},{11,1... | collective-permute-start | bytes 98312 | tf_op jit(solution)/shard_map/while/body/eval_jaxpr/ppermute | solution.py:22
  259.8 1.6 collective-permute-done.1
  261.9 1.9 collective-permute-start
  263.8 7.3 %collective-permute-start.1 = (f32[1,16,512]{2,1,0:T(8,128)S(1)}, f32[1,16,512]{2,1,0:T(8,128)S(1)}, u32[]{:S(2)}, u32[]{:S(2)}) collective-permute-start(f32[1,16,512]{2,1,0:T(8,128)S(1)} %get-tuple-element.112), channel_id=1, source_target_pairs={{1,0},{2,1},{3,2},{4,3},{5,4},{6,5},{7,6},{8,7},{9,8},{10,9},{11,1... | collective-permute-start | bytes 98312 | tf_op jit(solution)/shard_map/while/body/eval_jaxpr/ppermute | solution.py:22
  271.1 1.6 collective-permute-done.1
  273.3 1.9 collective-permute-start
  275.2 7.3 %collective-permute-start.1 = (f32[1,16,512]{2,1,0:T(8,128)S(1)}, f32[1,16,512]{2,1,0:T(8,128)S(1)}, u32[]{:S(2)}, u32[]{:S(2)}) collective-permute-start(f32[1,16,512]{2,1,0:T(8,128)S(1)} %get-tuple-element.112), channel_id=1, source_target_pairs={{1,0},{2,1},{3,2},{4,3},{5,4},{6,5},{7,6},{8,7},{9,8},{10,9},{11,1... | collective-permute-start | bytes 98312 | tf_op jit(solution)/shard_map/while/body/eval_jaxpr/ppermute | solution.py:22
  282.5 1.6 collective-permute-done.1
  284.6 1.9 collective-permute-start
  286.6 7.3 %collective-permute-start.1 = (f32[1,16,512]{2,1,0:T(8,128)S(1)}, f32[1,16,512]{2,1,0:T(8,128)S(1)}, u32[]{:S(2)}, u32[]{:S(2)}) collective-permute-start(f32[1,16,512]{2,1,0:T(8,128)S(1)} %get-tuple-element.112), channel_id=1, source_target_pairs={{1,0},{2,1},{3,2},{4,3},{5,4},{6,5},{7,6},{8,7},{9,8},{10,9},{11,1... | collective-permute-start | bytes 98312 | tf_op jit(solution)/shard_map/while/body/eval_jaxpr/ppermute | solution.py:22
  293.8 1.6 collective-permute-done.1
  296.0 1.9 collective-permute-start
  297.9 7.3 %collective-permute-start.1 = (f32[1,16,512]{2,1,0:T(8,128)S(1)}, f32[1,16,512]{2,1,0:T(8,128)S(1)}, u32[]{:S(2)}, u32[]{:S(2)}) collective-permute-start(f32[1,16,512]{2,1,0:T(8,128)S(1)} %get-tuple-element.112), channel_id=1, source_target_pairs={{1,0},{2,1},{3,2},{4,3},{5,4},{6,5},{7,6},{8,7},{9,8},{10,9},{11,1... | collective-permute-start | bytes 98312 | tf_op jit(solution)/shard_map/while/body/eval_jaxpr/ppermute | solution.py:22
  305.2 1.6 collective-permute-done.1
  307.3 1.9 collective-permute-start
  309.3 7.3 %collective-permute-start.1 = (f32[1,16,512]{2,1,0:T(8,128)S(1)}, f32[1,16,512]{2,1,0:T(8,128)S(1)}, u32[]{:S(2)}, u32[]{:S(2)}) collective-permute-start(f32[1,16,512]{2,1,0:T(8,128)S(1)} %get-tuple-element.112), channel_id=1, source_target_pairs={{1,0},{2,1},{3,2},{4,3},{5,4},{6,5},{7,6},{8,7},{9,8},{10,9},{11,1... | collective-permute-start | bytes 98312 | tf_op jit(solution)/shard_map/while/body/eval_jaxpr/ppermute | solution.py:22
  316.6 1.6 collective-permute-done.1
  318.7 1.9 collective-permute-start
  320.6 7.3 %collective-permute-start.1 = (f32[1,16,512]{2,1,0:T(8,128)S(1)}, f32[1,16,512]{2,1,0:T(8,128)S(1)}, u32[]{:S(2)}, u32[]{:S(2)}) collective-permute-start(f32[1,16,512]{2,1,0:T(8,128)S(1)} %get-tuple-element.112), channel_id=1, source_target_pairs={{1,0},{2,1},{3,2},{4,3},{5,4},{6,5},{7,6},{8,7},{9,8},{10,9},{11,1... | collective-permute-start | bytes 98312 | tf_op jit(solution)/shard_map/while/body/eval_jaxpr/ppermute | solution.py:22
  327.9 1.6 collective-permute-done.1
  330.1 1.9 collective-permute-start
  332.0 7.3 %collective-permute-start.1 = (f32[1,16,512]{2,1,0:T(8,128)S(1)}, f32[1,16,512]{2,1,0:T(8,128)S(1)}, u32[]{:S(2)}, u32[]{:S(2)}) collective-permute-start(f32[1,16,512]{2,1,0:T(8,128)S(1)} %get-tuple-element.112), channel_id=1, source_target_pairs={{1,0},{2,1},{3,2},{4,3},{5,4},{6,5},{7,6},{8,7},{9,8},{10,9},{11,1... | collective-permute-start | bytes 98312 | tf_op jit(solution)/shard_map/while/body/eval_jaxpr/ppermute | solution.py:22
  339.3 1.6 collective-permute-done.1
  341.4 1.9 collective-permute-start
  343.4 7.3 %collective-permute-start.1 = (f32[1,16,512]{2,1,0:T(8,128)S(1)}, f32[1,16,512]{2,1,0:T(8,128)S(1)}, u32[]{:S(2)}, u32[]{:S(2)}) collective-permute-start(f32[1,16,512]{2,1,0:T(8,128)S(1)} %get-tuple-element.112), channel_id=1, source_target_pairs={{1,0},{2,1},{3,2},{4,3},{5,4},{6,5},{7,6},{8,7},{9,8},{10,9},{11,1... | collective-permute-start | bytes 98312 | tf_op jit(solution)/shard_map/while/body/eval_jaxpr/ppermute | solution.py:22
  350.6 1.6 collective-permute-done.1
  352.8 1.9 collective-permute-start
  354.7 7.3 %collective-permute-start.1 = (f32[1,16,512]{2,1,0:T(8,128)S(1)}, f32[1,16,512]{2,1,0:T(8,128)S(1)}, u32[]{:S(2)}, u32[]{:S(2)}) collective-permute-start(f32[1,16,512]{2,1,0:T(8,128)S(1)} %get-tuple-element.112), channel_id=1, source_target_pairs={{1,0},{2,1},{3,2},{4,3},{5,4},{6,5},{7,6},{8,7},{9,8},{10,9},{11,1... | collective-permute-start | bytes 98312 | tf_op jit(solution)/shard_map/while/body/eval_jaxpr/ppermute | solution.py:22
  364.1 1.9 collective-permute-start
  366.1 7.3 %collective-permute-start.1 = (f32[1,16,512]{2,1,0:T(8,128)S(1)}, f32[1,16,512]{2,1,0:T(8,128)S(1)}, u32[]{:S(2)}, u32[]{:S(2)}) collective-permute-start(f32[1,16,512]{2,1,0:T(8,128)S(1)} %get-tuple-element.112), channel_id=1, source_target_pairs={{1,0},{2,1},{3,2},{4,3},{5,4},{6,5},{7,6},{8,7},{9,8},{10,9},{11,1... | collective-permute-start | bytes 98312 | tf_op jit(solution)/shard_map/while/body/eval_jaxpr/ppermute | solution.py:22
  375.5 1.9 collective-permute-start
  377.4 7.3 %collective-permute-start.1 = (f32[1,16,512]{2,1,0:T(8,128)S(1)}, f32[1,16,512]{2,1,0:T(8,128)S(1)}, u32[]{:S(2)}, u32[]{:S(2)}) collective-permute-start(f32[1,16,512]{2,1,0:T(8,128)S(1)} %get-tuple-element.112), channel_id=1, source_target_pairs={{1,0},{2,1},{3,2},{4,3},{5,4},{6,5},{7,6},{8,7},{9,8},{10,9},{11,1... | collective-permute-start | bytes 98312 | tf_op jit(solution)/shard_map/while/body/eval_jaxpr/ppermute | solution.py:22
  386.9 1.9 collective-permute-start
  388.8 7.3 %collective-permute-start.1 = (f32[1,16,512]{2,1,0:T(8,128)S(1)}, f32[1,16,512]{2,1,0:T(8,128)S(1)}, u32[]{:S(2)}, u32[]{:S(2)}) collective-permute-start(f32[1,16,512]{2,1,0:T(8,128)S(1)} %get-tuple-element.112), channel_id=1, source_target_pairs={{1,0},{2,1},{3,2},{4,3},{5,4},{6,5},{7,6},{8,7},{9,8},{10,9},{11,1... | collective-permute-start | bytes 98312 | tf_op jit(solution)/shard_map/while/body/eval_jaxpr/ppermute | solution.py:22
  398.2 1.9 collective-permute-start
  400.2 7.3 %collective-permute-start.1 = (f32[1,16,512]{2,1,0:T(8,128)S(1)}, f32[1,16,512]{2,1,0:T(8,128)S(1)}, u32[]{:S(2)}, u32[]{:S(2)}) collective-permute-start(f32[1,16,512]{2,1,0:T(8,128)S(1)} %get-tuple-element.112), channel_id=1, source_target_pairs={{1,0},{2,1},{3,2},{4,3},{5,4},{6,5},{7,6},{8,7},{9,8},{10,9},{11,1... | collective-permute-start | bytes 98312 | tf_op jit(solution)/shard_map/while/body/eval_jaxpr/ppermute | solution.py:22
  409.6 1.9 collective-permute-start
  411.5 7.3 %collective-permute-start.1 = (f32[1,16,512]{2,1,0:T(8,128)S(1)}, f32[1,16,512]{2,1,0:T(8,128)S(1)}, u32[]{:S(2)}, u32[]{:S(2)}) collective-permute-start(f32[1,16,512]{2,1,0:T(8,128)S(1)} %get-tuple-element.112), channel_id=1, source_target_pairs={{1,0},{2,1},{3,2},{4,3},{5,4},{6,5},{7,6},{8,7},{9,8},{10,9},{11,1... | collective-permute-start | bytes 98312 | tf_op jit(solution)/shard_map/while/body/eval_jaxpr/ppermute | solution.py:22
  420.9 1.9 collective-permute-start
  422.9 7.3 %collective-permute-start.1 = (f32[1,16,512]{2,1,0:T(8,128)S(1)}, f32[1,16,512]{2,1,0:T(8,128)S(1)}, u32[]{:S(2)}, u32[]{:S(2)}) collective-permute-start(f32[1,16,512]{2,1,0:T(8,128)S(1)} %get-tuple-element.112), channel_id=1, source_target_pairs={{1,0},{2,1},{3,2},{4,3},{5,4},{6,5},{7,6},{8,7},{9,8},{10,9},{11,1... | collective-permute-start | bytes 98312 | tf_op jit(solution)/shard_map/while/body/eval_jaxpr/ppermute | solution.py:22
  432.3 1.9 collective-permute-start
  434.2 7.3 %collective-permute-start.1 = (f32[1,16,512]{2,1,0:T(8,128)S(1)}, f32[1,16,512]{2,1,0:T(8,128)S(1)}, u32[]{:S(2)}, u32[]{:S(2)}) collective-permute-start(f32[1,16,512]{2,1,0:T(8,128)S(1)} %get-tuple-element.112), channel_id=1, source_target_pairs={{1,0},{2,1},{3,2},{4,3},{5,4},{6,5},{7,6},{8,7},{9,8},{10,9},{11,1... | collective-permute-start | bytes 98312 | tf_op jit(solution)/shard_map/while/body/eval_jaxpr/ppermute | solution.py:22
  443.7 1.9 collective-permute-start
  445.6 7.3 %collective-permute-start.1 = (f32[1,16,512]{2,1,0:T(8,128)S(1)}, f32[1,16,512]{2,1,0:T(8,128)S(1)}, u32[]{:S(2)}, u32[]{:S(2)}) collective-permute-start(f32[1,16,512]{2,1,0:T(8,128)S(1)} %get-tuple-element.112), channel_id=1, source_target_pairs={{1,0},{2,1},{3,2},{4,3},{5,4},{6,5},{7,6},{8,7},{9,8},{10,9},{11,1... | collective-permute-start | bytes 98312 | tf_op jit(solution)/shard_map/while/body/eval_jaxpr/ppermute | solution.py:22
  455.0 1.9 collective-permute-start
  457.0 7.3 %collective-permute-start.1 = (f32[1,16,512]{2,1,0:T(8,128)S(1)}, f32[1,16,512]{2,1,0:T(8,128)S(1)}, u32[]{:S(2)}, u32[]{:S(2)}) collective-permute-start(f32[1,16,512]{2,1,0:T(8,128)S(1)} %get-tuple-element.112), channel_id=1, source_target_pairs={{1,0},{2,1},{3,2},{4,3},{5,4},{6,5},{7,6},{8,7},{9,8},{10,9},{11,1... | collective-permute-start | bytes 98312 | tf_op jit(solution)/shard_map/while/body/eval_jaxpr/ppermute | solution.py:22
  466.4 2.1 collective-permute-start.4
  468.4 7.3 %collective-permute-start.5 = (f32[1,16,512]{2,1,0:T(8,128)S(1)}, f32[1,16,512]{2,1,0:T(8,128)S(1)}, u32[]{:S(2)}, u32[]{:S(2)}) collective-permute-start(f32[1,16,512]{2,1,0:T(8,128)S(1)} %get-tuple-element.89), channel_id=1, source_target_pairs={{1,0},{2,1},{3,2},{4,3},{5,4},{6,5},{7,6},{8,7},{9,8},{10,9},{11,1... | collective-permute-start | bytes 98312 | tf_op jit(solution)/shard_map/ppermute | solution.py:22
  475.8 1.7 gather_fusion.1
  477.5 1.9 scatter_custom_fusion
  479.5 129.0 %all-reduce.4 = f32[4096]{0:T(1024)S(1)} all-reduce(f32[4096]{0:T(1024)S(1)} %scatter_custom_fusion), channel_id=3, replica_groups=mesh['dir'=16,'space'=32] {'space'}, use_global_device_ids=true, to_apply=%region_4.5.clone | all-reduce | flops 4096 | bytes 32768
  (162 shorter events, 37.4 us)
Async XLA Ops:
  7.2 0.8 copy-start.3
  7.2 119.9 %all-gather.3.cloned.1.call-start = ((), (), s32[]{:S(2)}) async-start(), calls=%async_computation | async-start | bytes 1622016 | tf_op jit(solution)/shard_map/all_gather | solution.py:99
  7.2 37.8 %copy-start.2 = (s32[1,8,512]{2,1,0:T(8,128)S(1)}, s32[1,8,512]{2,1,0:T(8,128)}, u32[]{:S(2)}) copy-start(s32[1,8,512]{2,1,0:T(8,128)} %param.13) | copy-start | bytes 49156
  7.2 39.8 %copy-start.7 = (s32[1,256]{1,0:T(1,128)S(1)}, s32[1,256]{1,0:T(1,128)}, u32[]{:S(2)}) copy-start(s32[1,256]{1,0:T(1,128)} %param.14) | copy-start | bytes 3076
  219.7 2.4 copy-start.1
  219.8 12.3 %copy-start.4 = (s32[1,256]{1,0:T(1,128)S(1)}, s32[1,256]{1,0:T(1,128)}, u32[]{:S(2)}) copy-start(s32[1,256]{1,0:T(1,128)} %param.16) | copy-start | bytes 3076
  219.8 12.3 %copy-start.5 = (s32[1,256,1]{1,2,0:T(1,128)S(1)}, s32[1,256,1]{1,2,0:T(1,128)}, u32[]{:S(2)}) copy-start(s32[1,256,1]{1,2,0:T(1,128)} %param.15) | copy-start | bytes 3076
  222.9 10.7 %collective-permute-start.2 = (f32[3,2,16,512]{3,2,1,0:T(8,128)S(1)}, f32[3,2,16,512]{3,2,1,0:T(8,128)S(1)}, u32[]{:S(2)}, u32[]{:S(2)}) collective-permute-start(f32[3,2,16,512]{3,2,1,0:T(8,128)S(1)} %get-tuple-element.84), channel_id=1, source_target_pairs={{0,1},{1,2},{2,3},{3,4},{4,5},{5,6},{6,7},{7,8},{8,9},{9,10},{10,1... | collective-permute-start | bytes 589832 | tf_op jit(solution)/shard_map/ppermute | solution.py:20
  224.9 10.3 %collective-permute-start.3 = (f32[3,2,16,512]{3,2,1,0:T(8,128)S(1)}, f32[3,2,16,512]{3,2,1,0:T(8,128)S(1)}, u32[]{:S(2)}, u32[]{:S(2)}) collective-permute-start(f32[3,2,16,512]{3,2,1,0:T(8,128)S(1)} %get-tuple-element.85), channel_id=1, source_target_pairs={{1,0},{2,1},{3,2},{4,3},{5,4},{6,5},{7,6},{8,7},{9,8},{10,9},{11,1... | collective-permute-start | bytes 589832 | tf_op jit(solution)/shard_map/ppermute | solution.py:22
  239.0 9.4 %collective-permute-start = (f32[1,16,512]{2,1,0:T(8,128)S(1)}, f32[1,16,512]{2,1,0:T(8,128)S(1)}, u32[]{:S(2)}, u32[]{:S(2)}) collective-permute-start(f32[1,16,512]{2,1,0:T(8,128)S(1)} %get-tuple-element.111), channel_id=1, source_target_pairs={{0,1},{1,2},{2,3},{3,4},{4,5},{5,6},{6,7},{7,8},{8,9},{9,10},{10,1... | collective-permute-start | bytes 98312 | tf_op jit(solution)/shard_map/while/body/eval_jaxpr/ppermute | solution.py:20
  241.1 8.9 %collective-permute-start.1 = (f32[1,16,512]{2,1,0:T(8,128)S(1)}, f32[1,16,512]{2,1,0:T(8,128)S(1)}, u32[]{:S(2)}, u32[]{:S(2)}) collective-permute-start(f32[1,16,512]{2,1,0:T(8,128)S(1)} %get-tuple-element.112), channel_id=1, source_target_pairs={{1,0},{2,1},{3,2},{4,3},{5,4},{6,5},{7,6},{8,7},{9,8},{10,9},{11,1... | collective-permute-start | bytes 98312 | tf_op jit(solution)/shard_map/while/body/eval_jaxpr/ppermute | solution.py:22
  250.5 9.2 %collective-permute-start = (f32[1,16,512]{2,1,0:T(8,128)S(1)}, f32[1,16,512]{2,1,0:T(8,128)S(1)}, u32[]{:S(2)}, u32[]{:S(2)}) collective-permute-start(f32[1,16,512]{2,1,0:T(8,128)S(1)} %get-tuple-element.111), channel_id=1, source_target_pairs={{0,1},{1,2},{2,3},{3,4},{4,5},{5,6},{6,7},{7,8},{8,9},{9,10},{10,1... | collective-permute-start | bytes 98312 | tf_op jit(solution)/shard_map/while/body/eval_jaxpr/ppermute | solution.py:20
  252.5 8.8 %collective-permute-start.1 = (f32[1,16,512]{2,1,0:T(8,128)S(1)}, f32[1,16,512]{2,1,0:T(8,128)S(1)}, u32[]{:S(2)}, u32[]{:S(2)}) collective-permute-start(f32[1,16,512]{2,1,0:T(8,128)S(1)} %get-tuple-element.112), channel_id=1, source_target_pairs={{1,0},{2,1},{3,2},{4,3},{5,4},{6,5},{7,6},{8,7},{9,8},{10,9},{11,1... | collective-permute-start | bytes 98312 | tf_op jit(solution)/shard_map/while/body/eval_jaxpr/ppermute | solution.py:22
  261.9 9.2 %collective-permute-start = (f32[1,16,512]{2,1,0:T(8,128)S(1)}, f32[1,16,512]{2,1,0:T(8,128)S(1)}, u32[]{:S(2)}, u32[]{:S(2)}) collective-permute-start(f32[1,16,512]{2,1,0:T(8,128)S(1)} %get-tuple-element.111), channel_id=1, source_target_pairs={{0,1},{1,2},{2,3},{3,4},{4,5},{5,6},{6,7},{7,8},{8,9},{9,10},{10,1... | collective-permute-start | bytes 98312 | tf_op jit(solution)/shard_map/while/body/eval_jaxpr/ppermute | solution.py:20
  263.8 8.8 %collective-permute-start.1 = (f32[1,16,512]{2,1,0:T(8,128)S(1)}, f32[1,16,512]{2,1,0:T(8,128)S(1)}, u32[]{:S(2)}, u32[]{:S(2)}) collective-permute-start(f32[1,16,512]{2,1,0:T(8,128)S(1)} %get-tuple-element.112), channel_id=1, source_target_pairs={{1,0},{2,1},{3,2},{4,3},{5,4},{6,5},{7,6},{8,7},{9,8},{10,9},{11,1... | collective-permute-start | bytes 98312 | tf_op jit(solution)/shard_map/while/body/eval_jaxpr/ppermute | solution.py:22
  273.3 9.2 %collective-permute-start = (f32[1,16,512]{2,1,0:T(8,128)S(1)}, f32[1,16,512]{2,1,0:T(8,128)S(1)}, u32[]{:S(2)}, u32[]{:S(2)}) collective-permute-start(f32[1,16,512]{2,1,0:T(8,128)S(1)} %get-tuple-element.111), channel_id=1, source_target_pairs={{0,1},{1,2},{2,3},{3,4},{4,5},{5,6},{6,7},{7,8},{8,9},{9,10},{10,1... | collective-permute-start | bytes 98312 | tf_op jit(solution)/shard_map/while/body/eval_jaxpr/ppermute | solution.py:20
  275.2 8.8 %collective-permute-start.1 = (f32[1,16,512]{2,1,0:T(8,128)S(1)}, f32[1,16,512]{2,1,0:T(8,128)S(1)}, u32[]{:S(2)}, u32[]{:S(2)}) collective-permute-start(f32[1,16,512]{2,1,0:T(8,128)S(1)} %get-tuple-element.112), channel_id=1, source_target_pairs={{1,0},{2,1},{3,2},{4,3},{5,4},{6,5},{7,6},{8,7},{9,8},{10,9},{11,1... | collective-permute-start | bytes 98312 | tf_op jit(solution)/shard_map/while/body/eval_jaxpr/ppermute | solution.py:22
  284.6 9.2 %collective-permute-start = (f32[1,16,512]{2,1,0:T(8,128)S(1)}, f32[1,16,512]{2,1,0:T(8,128)S(1)}, u32[]{:S(2)}, u32[]{:S(2)}) collective-permute-start(f32[1,16,512]{2,1,0:T(8,128)S(1)} %get-tuple-element.111), channel_id=1, source_target_pairs={{0,1},{1,2},{2,3},{3,4},{4,5},{5,6},{6,7},{7,8},{8,9},{9,10},{10,1... | collective-permute-start | bytes 98312 | tf_op jit(solution)/shard_map/while/body/eval_jaxpr/ppermute | solution.py:20
  286.6 8.8 %collective-permute-start.1 = (f32[1,16,512]{2,1,0:T(8,128)S(1)}, f32[1,16,512]{2,1,0:T(8,128)S(1)}, u32[]{:S(2)}, u32[]{:S(2)}) collective-permute-start(f32[1,16,512]{2,1,0:T(8,128)S(1)} %get-tuple-element.112), channel_id=1, source_target_pairs={{1,0},{2,1},{3,2},{4,3},{5,4},{6,5},{7,6},{8,7},{9,8},{10,9},{11,1... | collective-permute-start | bytes 98312 | tf_op jit(solution)/shard_map/while/body/eval_jaxpr/ppermute | solution.py:22
  296.0 9.2 %collective-permute-start = (f32[1,16,512]{2,1,0:T(8,128)S(1)}, f32[1,16,512]{2,1,0:T(8,128)S(1)}, u32[]{:S(2)}, u32[]{:S(2)}) collective-permute-start(f32[1,16,512]{2,1,0:T(8,128)S(1)} %get-tuple-element.111), channel_id=1, source_target_pairs={{0,1},{1,2},{2,3},{3,4},{4,5},{5,6},{6,7},{7,8},{8,9},{9,10},{10,1... | collective-permute-start | bytes 98312 | tf_op jit(solution)/shard_map/while/body/eval_jaxpr/ppermute | solution.py:20
  297.9 8.8 %collective-permute-start.1 = (f32[1,16,512]{2,1,0:T(8,128)S(1)}, f32[1,16,512]{2,1,0:T(8,128)S(1)}, u32[]{:S(2)}, u32[]{:S(2)}) collective-permute-start(f32[1,16,512]{2,1,0:T(8,128)S(1)} %get-tuple-element.112), channel_id=1, source_target_pairs={{1,0},{2,1},{3,2},{4,3},{5,4},{6,5},{7,6},{8,7},{9,8},{10,9},{11,1... | collective-permute-start | bytes 98312 | tf_op jit(solution)/shard_map/while/body/eval_jaxpr/ppermute | solution.py:22
  307.3 9.2 %collective-permute-start = (f32[1,16,512]{2,1,0:T(8,128)S(1)}, f32[1,16,512]{2,1,0:T(8,128)S(1)}, u32[]{:S(2)}, u32[]{:S(2)}) collective-permute-start(f32[1,16,512]{2,1,0:T(8,128)S(1)} %get-tuple-element.111), channel_id=1, source_target_pairs={{0,1},{1,2},{2,3},{3,4},{4,5},{5,6},{6,7},{7,8},{8,9},{9,10},{10,1... | collective-permute-start | bytes 98312 | tf_op jit(solution)/shard_map/while/body/eval_jaxpr/ppermute | solution.py:20
  309.3 8.8 %collective-permute-start.1 = (f32[1,16,512]{2,1,0:T(8,128)S(1)}, f32[1,16,512]{2,1,0:T(8,128)S(1)}, u32[]{:S(2)}, u32[]{:S(2)}) collective-permute-start(f32[1,16,512]{2,1,0:T(8,128)S(1)} %get-tuple-element.112), channel_id=1, source_target_pairs={{1,0},{2,1},{3,2},{4,3},{5,4},{6,5},{7,6},{8,7},{9,8},{10,9},{11,1... | collective-permute-start | bytes 98312 | tf_op jit(solution)/shard_map/while/body/eval_jaxpr/ppermute | solution.py:22
  318.7 9.2 %collective-permute-start = (f32[1,16,512]{2,1,0:T(8,128)S(1)}, f32[1,16,512]{2,1,0:T(8,128)S(1)}, u32[]{:S(2)}, u32[]{:S(2)}) collective-permute-start(f32[1,16,512]{2,1,0:T(8,128)S(1)} %get-tuple-element.111), channel_id=1, source_target_pairs={{0,1},{1,2},{2,3},{3,4},{4,5},{5,6},{6,7},{7,8},{8,9},{9,10},{10,1... | collective-permute-start | bytes 98312 | tf_op jit(solution)/shard_map/while/body/eval_jaxpr/ppermute | solution.py:20
  320.6 8.8 %collective-permute-start.1 = (f32[1,16,512]{2,1,0:T(8,128)S(1)}, f32[1,16,512]{2,1,0:T(8,128)S(1)}, u32[]{:S(2)}, u32[]{:S(2)}) collective-permute-start(f32[1,16,512]{2,1,0:T(8,128)S(1)} %get-tuple-element.112), channel_id=1, source_target_pairs={{1,0},{2,1},{3,2},{4,3},{5,4},{6,5},{7,6},{8,7},{9,8},{10,9},{11,1... | collective-permute-start | bytes 98312 | tf_op jit(solution)/shard_map/while/body/eval_jaxpr/ppermute | solution.py:22
  330.1 9.2 %collective-permute-start = (f32[1,16,512]{2,1,0:T(8,128)S(1)}, f32[1,16,512]{2,1,0:T(8,128)S(1)}, u32[]{:S(2)}, u32[]{:S(2)}) collective-permute-start(f32[1,16,512]{2,1,0:T(8,128)S(1)} %get-tuple-element.111), channel_id=1, source_target_pairs={{0,1},{1,2},{2,3},{3,4},{4,5},{5,6},{6,7},{7,8},{8,9},{9,10},{10,1... | collective-permute-start | bytes 98312 | tf_op jit(solution)/shard_map/while/body/eval_jaxpr/ppermute | solution.py:20
  332.0 8.8 %collective-permute-start.1 = (f32[1,16,512]{2,1,0:T(8,128)S(1)}, f32[1,16,512]{2,1,0:T(8,128)S(1)}, u32[]{:S(2)}, u32[]{:S(2)}) collective-permute-start(f32[1,16,512]{2,1,0:T(8,128)S(1)} %get-tuple-element.112), channel_id=1, source_target_pairs={{1,0},{2,1},{3,2},{4,3},{5,4},{6,5},{7,6},{8,7},{9,8},{10,9},{11,1... | collective-permute-start | bytes 98312 | tf_op jit(solution)/shard_map/while/body/eval_jaxpr/ppermute | solution.py:22
  341.4 9.2 %collective-permute-start = (f32[1,16,512]{2,1,0:T(8,128)S(1)}, f32[1,16,512]{2,1,0:T(8,128)S(1)}, u32[]{:S(2)}, u32[]{:S(2)}) collective-permute-start(f32[1,16,512]{2,1,0:T(8,128)S(1)} %get-tuple-element.111), channel_id=1, source_target_pairs={{0,1},{1,2},{2,3},{3,4},{4,5},{5,6},{6,7},{7,8},{8,9},{9,10},{10,1... | collective-permute-start | bytes 98312 | tf_op jit(solution)/shard_map/while/body/eval_jaxpr/ppermute | solution.py:20
  343.4 8.8 %collective-permute-start.1 = (f32[1,16,512]{2,1,0:T(8,128)S(1)}, f32[1,16,512]{2,1,0:T(8,128)S(1)}, u32[]{:S(2)}, u32[]{:S(2)}) collective-permute-start(f32[1,16,512]{2,1,0:T(8,128)S(1)} %get-tuple-element.112), channel_id=1, source_target_pairs={{1,0},{2,1},{3,2},{4,3},{5,4},{6,5},{7,6},{8,7},{9,8},{10,9},{11,1... | collective-permute-start | bytes 98312 | tf_op jit(solution)/shard_map/while/body/eval_jaxpr/ppermute | solution.py:22
  352.8 9.2 %collective-permute-start = (f32[1,16,512]{2,1,0:T(8,128)S(1)}, f32[1,16,512]{2,1,0:T(8,128)S(1)}, u32[]{:S(2)}, u32[]{:S(2)}) collective-permute-start(f32[1,16,512]{2,1,0:T(8,128)S(1)} %get-tuple-element.111), channel_id=1, source_target_pairs={{0,1},{1,2},{2,3},{3,4},{4,5},{5,6},{6,7},{7,8},{8,9},{9,10},{10,1... | collective-permute-start | bytes 98312 | tf_op jit(solution)/shard_map/while/body/eval_jaxpr/ppermute | solution.py:20
  354.7 8.8 %collective-permute-start.1 = (f32[1,16,512]{2,1,0:T(8,128)S(1)}, f32[1,16,512]{2,1,0:T(8,128)S(1)}, u32[]{:S(2)}, u32[]{:S(2)}) collective-permute-start(f32[1,16,512]{2,1,0:T(8,128)S(1)} %get-tuple-element.112), channel_id=1, source_target_pairs={{1,0},{2,1},{3,2},{4,3},{5,4},{6,5},{7,6},{8,7},{9,8},{10,9},{11,1... | collective-permute-start | bytes 98312 | tf_op jit(solution)/shard_map/while/body/eval_jaxpr/ppermute | solution.py:22
  364.1 9.2 %collective-permute-start = (f32[1,16,512]{2,1,0:T(8,128)S(1)}, f32[1,16,512]{2,1,0:T(8,128)S(1)}, u32[]{:S(2)}, u32[]{:S(2)}) collective-permute-start(f32[1,16,512]{2,1,0:T(8,128)S(1)} %get-tuple-element.111), channel_id=1, source_target_pairs={{0,1},{1,2},{2,3},{3,4},{4,5},{5,6},{6,7},{7,8},{8,9},{9,10},{10,1... | collective-permute-start | bytes 98312 | tf_op jit(solution)/shard_map/while/body/eval_jaxpr/ppermute | solution.py:20
  366.1 8.8 %collective-permute-start.1 = (f32[1,16,512]{2,1,0:T(8,128)S(1)}, f32[1,16,512]{2,1,0:T(8,128)S(1)}, u32[]{:S(2)}, u32[]{:S(2)}) collective-permute-start(f32[1,16,512]{2,1,0:T(8,128)S(1)} %get-tuple-element.112), channel_id=1, source_target_pairs={{1,0},{2,1},{3,2},{4,3},{5,4},{6,5},{7,6},{8,7},{9,8},{10,9},{11,1... | collective-permute-start | bytes 98312 | tf_op jit(solution)/shard_map/while/body/eval_jaxpr/ppermute | solution.py:22
  375.5 9.2 %collective-permute-start = (f32[1,16,512]{2,1,0:T(8,128)S(1)}, f32[1,16,512]{2,1,0:T(8,128)S(1)}, u32[]{:S(2)}, u32[]{:S(2)}) collective-permute-start(f32[1,16,512]{2,1,0:T(8,128)S(1)} %get-tuple-element.111), channel_id=1, source_target_pairs={{0,1},{1,2},{2,3},{3,4},{4,5},{5,6},{6,7},{7,8},{8,9},{9,10},{10,1... | collective-permute-start | bytes 98312 | tf_op jit(solution)/shard_map/while/body/eval_jaxpr/ppermute | solution.py:20
  377.4 8.8 %collective-permute-start.1 = (f32[1,16,512]{2,1,0:T(8,128)S(1)}, f32[1,16,512]{2,1,0:T(8,128)S(1)}, u32[]{:S(2)}, u32[]{:S(2)}) collective-permute-start(f32[1,16,512]{2,1,0:T(8,128)S(1)} %get-tuple-element.112), channel_id=1, source_target_pairs={{1,0},{2,1},{3,2},{4,3},{5,4},{6,5},{7,6},{8,7},{9,8},{10,9},{11,1... | collective-permute-start | bytes 98312 | tf_op jit(solution)/shard_map/while/body/eval_jaxpr/ppermute | solution.py:22
  386.9 9.2 %collective-permute-start = (f32[1,16,512]{2,1,0:T(8,128)S(1)}, f32[1,16,512]{2,1,0:T(8,128)S(1)}, u32[]{:S(2)}, u32[]{:S(2)}) collective-permute-start(f32[1,16,512]{2,1,0:T(8,128)S(1)} %get-tuple-element.111), channel_id=1, source_target_pairs={{0,1},{1,2},{2,3},{3,4},{4,5},{5,6},{6,7},{7,8},{8,9},{9,10},{10,1... | collective-permute-start | bytes 98312 | tf_op jit(solution)/shard_map/while/body/eval_jaxpr/ppermute | solution.py:20
  388.8 8.8 %collective-permute-start.1 = (f32[1,16,512]{2,1,0:T(8,128)S(1)}, f32[1,16,512]{2,1,0:T(8,128)S(1)}, u32[]{:S(2)}, u32[]{:S(2)}) collective-permute-start(f32[1,16,512]{2,1,0:T(8,128)S(1)} %get-tuple-element.112), channel_id=1, source_target_pairs={{1,0},{2,1},{3,2},{4,3},{5,4},{6,5},{7,6},{8,7},{9,8},{10,9},{11,1... | collective-permute-start | bytes 98312 | tf_op jit(solution)/shard_map/while/body/eval_jaxpr/ppermute | solution.py:22
  398.2 9.2 %collective-permute-start = (f32[1,16,512]{2,1,0:T(8,128)S(1)}, f32[1,16,512]{2,1,0:T(8,128)S(1)}, u32[]{:S(2)}, u32[]{:S(2)}) collective-permute-start(f32[1,16,512]{2,1,0:T(8,128)S(1)} %get-tuple-element.111), channel_id=1, source_target_pairs={{0,1},{1,2},{2,3},{3,4},{4,5},{5,6},{6,7},{7,8},{8,9},{9,10},{10,1... | collective-permute-start | bytes 98312 | tf_op jit(solution)/shard_map/while/body/eval_jaxpr/ppermute | solution.py:20
  400.2 8.8 %collective-permute-start.1 = (f32[1,16,512]{2,1,0:T(8,128)S(1)}, f32[1,16,512]{2,1,0:T(8,128)S(1)}, u32[]{:S(2)}, u32[]{:S(2)}) collective-permute-start(f32[1,16,512]{2,1,0:T(8,128)S(1)} %get-tuple-element.112), channel_id=1, source_target_pairs={{1,0},{2,1},{3,2},{4,3},{5,4},{6,5},{7,6},{8,7},{9,8},{10,9},{11,1... | collective-permute-start | bytes 98312 | tf_op jit(solution)/shard_map/while/body/eval_jaxpr/ppermute | solution.py:22
  409.6 9.2 %collective-permute-start = (f32[1,16,512]{2,1,0:T(8,128)S(1)}, f32[1,16,512]{2,1,0:T(8,128)S(1)}, u32[]{:S(2)}, u32[]{:S(2)}) collective-permute-start(f32[1,16,512]{2,1,0:T(8,128)S(1)} %get-tuple-element.111), channel_id=1, source_target_pairs={{0,1},{1,2},{2,3},{3,4},{4,5},{5,6},{6,7},{7,8},{8,9},{9,10},{10,1... | collective-permute-start | bytes 98312 | tf_op jit(solution)/shard_map/while/body/eval_jaxpr/ppermute | solution.py:20
  411.5 8.8 %collective-permute-start.1 = (f32[1,16,512]{2,1,0:T(8,128)S(1)}, f32[1,16,512]{2,1,0:T(8,128)S(1)}, u32[]{:S(2)}, u32[]{:S(2)}) collective-permute-start(f32[1,16,512]{2,1,0:T(8,128)S(1)} %get-tuple-element.112), channel_id=1, source_target_pairs={{1,0},{2,1},{3,2},{4,3},{5,4},{6,5},{7,6},{8,7},{9,8},{10,9},{11,1... | collective-permute-start | bytes 98312 | tf_op jit(solution)/shard_map/while/body/eval_jaxpr/ppermute | solution.py:22
  420.9 9.2 %collective-permute-start = (f32[1,16,512]{2,1,0:T(8,128)S(1)}, f32[1,16,512]{2,1,0:T(8,128)S(1)}, u32[]{:S(2)}, u32[]{:S(2)}) collective-permute-start(f32[1,16,512]{2,1,0:T(8,128)S(1)} %get-tuple-element.111), channel_id=1, source_target_pairs={{0,1},{1,2},{2,3},{3,4},{4,5},{5,6},{6,7},{7,8},{8,9},{9,10},{10,1... | collective-permute-start | bytes 98312 | tf_op jit(solution)/shard_map/while/body/eval_jaxpr/ppermute | solution.py:20
  422.9 8.8 %collective-permute-start.1 = (f32[1,16,512]{2,1,0:T(8,128)S(1)}, f32[1,16,512]{2,1,0:T(8,128)S(1)}, u32[]{:S(2)}, u32[]{:S(2)}) collective-permute-start(f32[1,16,512]{2,1,0:T(8,128)S(1)} %get-tuple-element.112), channel_id=1, source_target_pairs={{1,0},{2,1},{3,2},{4,3},{5,4},{6,5},{7,6},{8,7},{9,8},{10,9},{11,1... | collective-permute-start | bytes 98312 | tf_op jit(solution)/shard_map/while/body/eval_jaxpr/ppermute | solution.py:22
  432.3 9.2 %collective-permute-start = (f32[1,16,512]{2,1,0:T(8,128)S(1)}, f32[1,16,512]{2,1,0:T(8,128)S(1)}, u32[]{:S(2)}, u32[]{:S(2)}) collective-permute-start(f32[1,16,512]{2,1,0:T(8,128)S(1)} %get-tuple-element.111), channel_id=1, source_target_pairs={{0,1},{1,2},{2,3},{3,4},{4,5},{5,6},{6,7},{7,8},{8,9},{9,10},{10,1... | collective-permute-start | bytes 98312 | tf_op jit(solution)/shard_map/while/body/eval_jaxpr/ppermute | solution.py:20
  434.2 8.8 %collective-permute-start.1 = (f32[1,16,512]{2,1,0:T(8,128)S(1)}, f32[1,16,512]{2,1,0:T(8,128)S(1)}, u32[]{:S(2)}, u32[]{:S(2)}) collective-permute-start(f32[1,16,512]{2,1,0:T(8,128)S(1)} %get-tuple-element.112), channel_id=1, source_target_pairs={{1,0},{2,1},{3,2},{4,3},{5,4},{6,5},{7,6},{8,7},{9,8},{10,9},{11,1... | collective-permute-start | bytes 98312 | tf_op jit(solution)/shard_map/while/body/eval_jaxpr/ppermute | solution.py:22
  443.7 9.2 %collective-permute-start = (f32[1,16,512]{2,1,0:T(8,128)S(1)}, f32[1,16,512]{2,1,0:T(8,128)S(1)}, u32[]{:S(2)}, u32[]{:S(2)}) collective-permute-start(f32[1,16,512]{2,1,0:T(8,128)S(1)} %get-tuple-element.111), channel_id=1, source_target_pairs={{0,1},{1,2},{2,3},{3,4},{4,5},{5,6},{6,7},{7,8},{8,9},{9,10},{10,1... | collective-permute-start | bytes 98312 | tf_op jit(solution)/shard_map/while/body/eval_jaxpr/ppermute | solution.py:20
  445.6 8.8 %collective-permute-start.1 = (f32[1,16,512]{2,1,0:T(8,128)S(1)}, f32[1,16,512]{2,1,0:T(8,128)S(1)}, u32[]{:S(2)}, u32[]{:S(2)}) collective-permute-start(f32[1,16,512]{2,1,0:T(8,128)S(1)} %get-tuple-element.112), channel_id=1, source_target_pairs={{1,0},{2,1},{3,2},{4,3},{5,4},{6,5},{7,6},{8,7},{9,8},{10,9},{11,1... | collective-permute-start | bytes 98312 | tf_op jit(solution)/shard_map/while/body/eval_jaxpr/ppermute | solution.py:22
  455.0 9.2 %collective-permute-start = (f32[1,16,512]{2,1,0:T(8,128)S(1)}, f32[1,16,512]{2,1,0:T(8,128)S(1)}, u32[]{:S(2)}, u32[]{:S(2)}) collective-permute-start(f32[1,16,512]{2,1,0:T(8,128)S(1)} %get-tuple-element.111), channel_id=1, source_target_pairs={{0,1},{1,2},{2,3},{3,4},{4,5},{5,6},{6,7},{7,8},{8,9},{9,10},{10,1... | collective-permute-start | bytes 98312 | tf_op jit(solution)/shard_map/while/body/eval_jaxpr/ppermute | solution.py:20
  457.0 8.8 %collective-permute-start.1 = (f32[1,16,512]{2,1,0:T(8,128)S(1)}, f32[1,16,512]{2,1,0:T(8,128)S(1)}, u32[]{:S(2)}, u32[]{:S(2)}) collective-permute-start(f32[1,16,512]{2,1,0:T(8,128)S(1)} %get-tuple-element.112), channel_id=1, source_target_pairs={{1,0},{2,1},{3,2},{4,3},{5,4},{6,5},{7,6},{8,7},{9,8},{10,9},{11,1... | collective-permute-start | bytes 98312 | tf_op jit(solution)/shard_map/while/body/eval_jaxpr/ppermute | solution.py:22
  466.3 143.2 %copy-start = (f32[8,16,512]{2,1,0:T(8,128)}, f32[8,16,512]{2,1,0:T(8,128)S(1)}, u32[]{:S(2)}) copy-start(f32[8,16,512]{2,1,0:T(8,128)S(1)} %get-tuple-element.56) | copy-start | bytes 786436
  466.3 11.2 %copy-start.6 = (f32[1,256]{1,0:T(1,128)S(1)}, f32[1,256]{1,0:T(1,128)}, u32[]{:S(2)}) copy-start(f32[1,256]{1,0:T(1,128)} %param.17) | copy-start | bytes 3076
  466.4 142.7 %collective-permute-start.4 = (f32[1,16,512]{2,1,0:T(8,128)S(1)}, f32[1,16,512]{2,1,0:T(8,128)S(1)}, u32[]{:S(2)}, u32[]{:S(2)}) collective-permute-start(f32[1,16,512]{2,1,0:T(8,128)S(1)} %get-tuple-element.88), channel_id=1, source_target_pairs={{0,1},{1,2},{2,3},{3,4},{4,5},{5,6},{6,7},{7,8},{8,9},{9,10},{10,1... | collective-permute-start | bytes 98312 | tf_op jit(solution)/shard_map/ppermute | solution.py:20
  468.4 140.6 %collective-permute-start.5 = (f32[1,16,512]{2,1,0:T(8,128)S(1)}, f32[1,16,512]{2,1,0:T(8,128)S(1)}, u32[]{:S(2)}, u32[]{:S(2)}) collective-permute-start(f32[1,16,512]{2,1,0:T(8,128)S(1)} %get-tuple-element.89), channel_id=1, source_target_pairs={{1,0},{2,1},{3,2},{4,3},{5,4},{6,5},{7,6},{8,7},{9,8},{10,9},{11,1... | collective-permute-start | bytes 98312 | tf_op jit(solution)/shard_map/ppermute | solution.py:22
Sparse Core Ops, SparseCore 0:
  45.1 81.8 all-gather.2
